TPU v7x, 512 devices: a whole 4x8x8 slice. The times are simulated.
512 devices in a mesh: dp: 16 (over y, core), expert: 32 (over x, z).
Axes of the slice: x: 4, y: 8, z: 8, core: 2. Of those that a mesh axis runs over, the one named last changes fastest.
Arguments:
- tokens: bfloat16 [65536, 2048], P(('dp', 'expert')), may hold values from -24 to 24
- out_grad: bfloat16 [65536, 2048], P(('dp', 'expert')), may hold values from -3 to 3
- expert_ids: int32 [65536, 2], P(('dp', 'expert')), may hold values from 0 to 31, as said below
- route_probs: bfloat16 [65536, 2], P(('dp', 'expert')), may hold values from 0.099609375 to 0.8984375
- gate_weight: bfloat16 [32, 2048, 384], P('expert', 'dp'), may hold values from -0.125 to 0.125
- up_weight: bfloat16 [32, 2048, 384], P('expert', 'dp'), may hold values from -0.125 to 0.125
- down_weight: bfloat16 [32, 384, 2048], P('expert', None, 'dp'), may hold values from -0.3125 to 0.3125
- gate_mask: int32 [32, 512, 384], P('expert', 'dp'), may hold values from 0 to 5
- up_mask: int32 [32, 512, 384], P('expert', 'dp'), may hold values from 0 to 5
- down_mask: int32 [32, 96, 2048], P('expert', None, 'dp'), may hold values from 0 to 5
Outputs:
- token_grad: bfloat16 [65536, 2048], P(('dp', 'expert'))
- prob_grad: bfloat16 [65536, 2], P(('dp', 'expert'))
- gate_grad: float32 [32, 2048, 384], P('expert', 'dp')
- up_grad: float32 [32, 2048, 384], P('expert', 'dp')
Inputs may be any that keep to these rules, and one draw needn't show every extreme that they name: `expert_ids`: each row names 2 different experts. The rows of one device name no expert more than 12 times; in every draw some expert is named exactly 12 times by the rows of every device of some data group.
All inputs are finite; a program needn't handle non-finite values.
Results may differ from a plain program's by a relative error of at most 0.02.
Values may be sent and summed in bfloat16 or wider, within the bound.
No kernel may reach another device: no remote copies, remote signals or barrier semaphores. Data moves between devices by JAX's collectives and lax.ppermute only.
A program may use at most 64 MiB of HBM per device.

v0:
```python
import jax
import jax.numpy as jnp
import numpy as np
from jax import lax
from jax.sharding import PartitionSpec as P

decay_rate = 24.0
pair_table = np.array(
    [[1, 1, 0, 0], [1, 0, 1, 0], [1, 0, 0, 1], [0, 1, 1, 0], [0, 1, 0, 1], [0, 0, 1, 1]], np.float32
)


def expand_pattern(pattern):
    group_count, col_count = pattern.shape
    picked = (pattern[None, :, :] == jnp.arange(6, dtype=jnp.int32)[:, None, None]).astype(
        jnp.float32
    )
    keeps = jnp.einsum("pgc,pj->gjc", picked, jnp.asarray(pair_table, jnp.float32))
    return keeps.reshape(group_count * 4, col_count)


def per_device(
    tokens,
    out_grad,
    expert_ids,
    route_probs,
    gate_weight,
    up_weight,
    down_weight,
    gate_mask,
    up_mask,
    down_mask,
):
    row_count, model_width = tokens.shape
    top_count = expert_ids.shape[1]
    expert_count = lax.axis_size("expert")
    capacity = 3 * row_count * top_count // (2 * expert_count)
    slot_total = expert_count * capacity
    keep_gate = expand_pattern(gate_mask[0])
    keep_up = expand_pattern(up_mask[0])
    keep_down = expand_pattern(down_mask[0])
    local_gate = (gate_weight[0] * keep_gate).astype(jnp.bfloat16)
    local_up = (up_weight[0] * keep_up).astype(jnp.bfloat16)
    local_down = (down_weight[0] * keep_down).astype(jnp.bfloat16)
    gathered_gate = lax.all_gather(local_gate, "dp", axis=0, tiled=True)
    gathered_up = lax.all_gather(local_up, "dp", axis=0, tiled=True)
    gathered_down = lax.all_gather(local_down, "dp", axis=1, tiled=True)
    flat_ids = expert_ids.reshape(-1)
    onehot = (flat_ids[:, None] == jnp.arange(expert_count, dtype=jnp.int32)[None, :]).astype(
        jnp.int32
    )
    earlier = jnp.cumsum(onehot, axis=0) - onehot
    slot_index = jnp.sum(earlier * onehot, axis=1)
    target = (flat_ids * capacity + slot_index).reshape(row_count, top_count)
    chosen = target.T[:, None, :] == jnp.arange(slot_total, dtype=jnp.int32)[None, :, None]
    chosen_float = chosen.astype(jnp.float32)
    placing = jnp.sum(chosen_float, axis=0).astype(jnp.bfloat16)
    send_rows = jnp.dot(placing, tokens, preferred_element_type=jnp.float32).astype(jnp.bfloat16)
    send_grads = jnp.dot(placing, out_grad, preferred_element_type=jnp.float32).astype(jnp.bfloat16)
    send_probs = jnp.einsum("kst,tk->s", chosen_float, route_probs.astype(jnp.float32)).astype(
        jnp.bfloat16
    )
    arrived_rows, arrived_grads, arrived_probs = (
        lax.all_to_all(
            send_rows.reshape(expert_count, capacity, model_width),
            "expert",
            split_axis=0,
            concat_axis=0,
            tiled=True,
        ),
        lax.all_to_all(
            send_grads.reshape(expert_count, capacity, model_width),
            "expert",
            split_axis=0,
            concat_axis=0,
            tiled=True,
        ),
        lax.all_to_all(
            send_probs.reshape(expert_count, capacity),
            "expert",
            split_axis=0,
            concat_axis=0,
            tiled=True,
        ),
    )
    inputs = arrived_rows.reshape(slot_total, model_width)
    cotan = arrived_grads.reshape(slot_total, model_width)
    probs = arrived_probs.reshape(slot_total)
    gate_pre = jnp.dot(inputs, gathered_gate, preferred_element_type=jnp.float32)
    up_pre = jnp.dot(inputs, gathered_up, preferred_element_type=jnp.float32)
    sigmoid_val = jax.nn.sigmoid(gate_pre)
    silu_val = gate_pre * sigmoid_val
    hidden = (silu_val * up_pre).astype(jnp.bfloat16)
    expert_out = jnp.dot(hidden, gathered_down, preferred_element_type=jnp.float32)
    prob_slot = jnp.sum(expert_out * cotan.astype(jnp.float32), axis=1).astype(jnp.bfloat16)
    weighted = (probs.astype(jnp.float32)[:, None] * cotan.astype(jnp.float32)).astype(jnp.bfloat16)
    hidden_grad = jnp.einsum(
        "rd,hd->rh", weighted, gathered_down, preferred_element_type=jnp.float32
    )
    gate_delta = (
        hidden_grad * up_pre * sigmoid_val * (1.0 + gate_pre * (1.0 - sigmoid_val))
    ).astype(jnp.bfloat16)
    up_delta = (hidden_grad * silu_val).astype(jnp.bfloat16)
    slot_grad = (
        jnp.einsum("rh,dh->rd", gate_delta, gathered_gate, preferred_element_type=jnp.float32)
        + jnp.einsum("rh,dh->rd", up_delta, gathered_up, preferred_element_type=jnp.float32)
    ).astype(jnp.bfloat16)
    back_grad, back_prob = (
        lax.all_to_all(
            slot_grad.reshape(expert_count, capacity, model_width),
            "expert",
            split_axis=0,
            concat_axis=0,
            tiled=True,
        ),
        lax.all_to_all(
            prob_slot.reshape(expert_count, capacity),
            "expert",
            split_axis=0,
            concat_axis=0,
            tiled=True,
        ),
    )
    token_grad = jnp.einsum(
        "st,sd->td",
        placing,
        back_grad.reshape(slot_total, model_width),
        preferred_element_type=jnp.float32,
    ).astype(jnp.bfloat16)
    prob_grad = jnp.einsum(
        "kst,s->tk", chosen_float, back_prob.reshape(slot_total).astype(jnp.float32)
    ).astype(jnp.bfloat16)
    part_gate = jnp.einsum("rd,rh->dh", inputs, gate_delta, preferred_element_type=jnp.float32)
    part_up = jnp.einsum("rd,rh->dh", inputs, up_delta, preferred_element_type=jnp.float32)
    share_rows = gate_weight.shape[1]
    total_gate, total_up = (
        lax.psum(part_gate.astype(jnp.bfloat16), "dp").astype(jnp.float32),
        lax.psum(part_up.astype(jnp.bfloat16), "dp").astype(jnp.float32),
    )
    row_start = lax.axis_index("dp") * share_rows
    share_gate = lax.dynamic_slice_in_dim(total_gate, row_start, share_rows, 0)
    share_up = lax.dynamic_slice_in_dim(total_up, row_start, share_rows, 0)
    gate_grad = (share_gate + decay_rate * (1.0 - keep_gate) * gate_weight[0].astype(jnp.float32))[
        None
    ]
    up_grad = (share_up + decay_rate * (1.0 - keep_up) * up_weight[0].astype(jnp.float32))[None]
    return (token_grad, prob_grad, gate_grad, up_grad)


def solution(mesh):
    placed = (
        P(("dp", "expert"), None),
        P(("dp", "expert"), None),
        P(("dp", "expert"), None),
        P(("dp", "expert"), None),
        P("expert", "dp", None),
        P("expert", "dp", None),
        P("expert", None, "dp"),
        P("expert", "dp", None),
        P("expert", "dp", None),
        P("expert", None, "dp"),
    )
    return jax.shard_map(
        per_device,
        mesh=mesh,
        in_specs=placed,
        out_specs=(
            P(("dp", "expert"), None),
            P(("dp", "expert"), None),
            P("expert", "dp", None),
            P("expert", "dp", None),
        ),
        check_vma=False,
    )
```

profile of v0, /device:TPU:1, one launch (start us, length us, event | category | flops | bytes accessed | tf_op | source)
XLA Modules:
  0.0 328.2 jit_solution(18292256265993113642)
XLA Ops:
  8.4 1.6 fusion.5
  13.1 13.7 %all-to-all-start = ((bf16[32,1,12]{2,1,0:T(2,128)(2,1)}), bf16[32,1,12]{2,1,0:T(2,128)(2,1)S(1)}, u32[]{:S(2)}, u32[]{:S(2)}) async-start(bf16[32,1,12]{2,1,0:T(2,128)(2,1)} %all_to_all.25), calls=%async_computation | async-start | bytes 32768 | tf_op jit(solution)/shard_map/all_to_all | solution.py:78
  27.5 1.5 reshape.97
  29.0 6.4 %all-to-all-done = bf16[32,1,12]{2,1,0:T(2,128)(2,1)S(1)} async-done(((bf16[32,1,12]{2,1,0:T(2,128)(2,1)}), bf16[32,1,12]{2,1,0:T(2,128)(2,1)S(1)}, u32[]{:S(2)}, u32[]{:S(2)}) %all-to-all-start) | async-done | bytes 800 | tf_op jit(solution)/shard_map/all_to_all | solution.py:78
  35.4 4.0 %all-to-all-start.2 = ((bf16[32,12,2048]{2,1,0:T(8,128)(2,1)}), bf16[32,12,2048]{2,1,0:T(8,128)(2,1)S(1)}, u32[]{:S(2)}, u32[]{:S(2)}) async-start(bf16[32,12,2048]{2,1,0:T(8,128)(2,1)} %reshape.97), calls=%async_computation.2 | async-start | bytes 4194304 | tf_op jit(solution)/shard_map/all_to_all | solution.py:64
  40.5 2.8 convolution_convert_fusion.3
  43.3 3.6 %reshape.95 = bf16[32,12,2048]{2,1,0:T(8,128)(2,1)} reshape(bf16[384,2048]{1,0:T(8,128)(2,1)} %convolution_convert_fusion.3) | data formatting | bytes 3145728 | tf_op jit(solution)/shard_map/reshape | solution.py:72
  46.9 41.9 %all-to-all-done.2 = bf16[32,12,2048]{2,1,0:T(8,128)(2,1)S(1)} async-done(((bf16[32,12,2048]{2,1,0:T(8,128)(2,1)}), bf16[32,12,2048]{2,1,0:T(8,128)(2,1)S(1)}, u32[]{:S(2)}, u32[]{:S(2)}) %all-to-all-start.2) | async-done | bytes 1572896 | tf_op jit(solution)/shard_map/all_to_all | solution.py:64
  88.8 6.3 %all-to-all-start.1 = ((bf16[32,12,2048]{2,1,0:T(8,128)(2,1)}), bf16[32,12,2048]{2,1,0:T(8,128)(2,1)}, u32[]{:S(2)}, u32[]{:S(2)}) async-start(bf16[32,12,2048]{2,1,0:T(8,128)(2,1)} %reshape.95), calls=%async_computation.1 | async-start | bytes 4194304 | tf_op jit(solution)/shard_map/all_to_all | solution.py:71
  96.2 1.4 reshape.98
  97.6 46.8 %all-to-all-done.1 = bf16[32,12,2048]{2,1,0:T(8,128)(2,1)} async-done(((bf16[32,12,2048]{2,1,0:T(8,128)(2,1)}), bf16[32,12,2048]{2,1,0:T(8,128)(2,1)}, u32[]{:S(2)}, u32[]{:S(2)}) %all-to-all-start.1) | async-done | bytes 1572896 | tf_op jit(solution)/shard_map/all_to_all | solution.py:71
  144.4 3.9 %reshape.105 = f32[384,2048]{1,0:T(8,128)} reshape(bf16[32,12,2048]{2,1,0:T(8,128)(2,1)} %all-to-all-done.1) | data formatting | bytes 4718592 | tf_op jit(solution)/shard_map/convert_element_type | solution.py:96
  148.4 3.2 fusion.28
  151.6 3.2 fusion.27
  154.7 3.9 %multiply_reduce_fusion = bf16[384]{0:T(512)(128)(2,1)S(1)} fusion(f32[384,2048]{1,0:T(8,128)} %reshape.105, bf16[384,2048]{1,0:T(8,128)(2,1)} %all-gather.4.cloned.1.call-done, f32[384,384]{1,0:T(8,128)} %fusion.27, f32[384,384]{1,0:T(8,128)} %fusion.28), kind=kOutput, calls=%fused_computation | convolution fusion | flops 606436992 | bytes 5899008 | tf_op jit(solution)/shard_map/dot_general | solution.py:94
  159.4 6.3 %all-to-all-start.4 = ((bf16[32,1,12]{2,1,0:T(2,128)(2,1)}), bf16[32,1,12]{2,1,0:T(2,128)(2,1)S(1)}, u32[]{:S(2)}, u32[]{:S(2)}) async-start(bf16[32,1,12]{2,1,0:T(2,128)(2,1)} %convert_element_type.162), calls=%async_computation.4 | async-start | bytes 32768 | tf_op jit(solution)/shard_map/all_to_all | solution.py:116
  165.8 3.5 %multiply_convert_fusion.3 = (bf16[384,384]{1,0:T(8,128)(2,1)S(1)}, bf16[384,384]{1,0:T(8,128)(2,1)S(1)}) fusion(f32[384,384]{1,0:T(8,128)} %fusion.28, f32[384,384]{1,0:T(8,128)} %fusion.27, bf16[384,2048]{1,0:T(8,128)(2,1)S(1)} %copy-done.15, f32[384,2048]{1,0:T(8,128)} %reshape.105, f32[384]{0:T(512)S(1)} %reshape.104), kind=kOutput, calls=%fused_computation.14 | convolution fusion | flops 607469568 | bytes 6489600 | tf_op jit(solution)/shard_map/rd,hd->rh/dot_general | solution.py:97
  171.9 1.5 reshape.101
  174.3 8.4 %all-to-all-start.3 = ((bf16[32,12,2048]{2,1,0:T(8,128)(2,1)}), bf16[32,12,2048]{2,1,0:T(8,128)(2,1)S(1)}, u32[]{:S(2)}, u32[]{:S(2)}) async-start(bf16[32,12,2048]{2,1,0:T(8,128)(2,1)} %reshape.101), calls=%async_computation.3 | async-start | bytes 4194304 | tf_op jit(solution)/shard_map/all_to_all | solution.py:109
  182.9 3.9 %convolution_convert_fusion = bf16[2048,384]{1,0:T(8,128)(2,1)} fusion(bf16[384,2048]{1,0:T(8,128)(2,1)} %reshape.98, bf16[384,384]{1,0:T(8,128)(2,1)} %copy-done.9), kind=kOutput, calls=%fused_computation.3 | convolution fusion | flops 604766208 | bytes 3440640 | tf_op jit(solution)/shard_map/rd,rh->dh/dot_general | solution.py:134
  186.8 2.4 convolution_convert_fusion.1
  190.1 125.8 %all-reduce.3.cloned.1.call-done = (bf16[2048,384]{1,0:T(8,128)(2,1)}, bf16[2048,384]{1,0:T(8,128)(2,1)}) async-done(((bf16[2048,384]{1,0:T(8,128)(2,1)}, bf16[2048,384]{1,0:T(8,128)(2,1)}), (bf16[2048,384]{1,0:T(8,128)(2,1)}, bf16[2048,384]{1,0:T(8,128)(2,1)})) %all-reduce.3.cloned.1.call-update) | async-done | bytes 3145744 | tf_op jit(solution)/shard_map/psum | solution.py:137
  315.9 1.8 fusion.7
  319.0 2.7 convolution_convert_fusion.4
  (80 shorter events, 13.7 us)
Async XLA Ops:
  7.2 19.8 %copy-start = (bf16[128,2048]{1,0:T(8,128)(2,1)S(1)}, bf16[128,2048]{1,0:T(8,128)(2,1)}, u32[]{:S(2)}) copy-start(bf16[128,2048]{1,0:T(8,128)(2,1)} %param.13) | copy-start | bytes 1572868
  7.2 5.0 %copy-start.14 = (s32[128,2]{0,1:T(2,128)S(1)}, s32[128,2]{0,1:T(2,128)}, u32[]{:S(2)}) copy-start(s32[128,2]{0,1:T(2,128)} %param.15) | copy-start | bytes 3076
  7.2 5.0 %copy-start.16 = (bf16[128,2]{0,1:T(2,128)(2,1)S(1)}, bf16[128,2]{0,1:T(2,128)(2,1)}, u32[]{:S(2)}) copy-start(bf16[128,2]{0,1:T(2,128)(2,1)} %param.16) | copy-start | bytes 1540
  7.2 141.2 %all-gather.8.cloned.1.call-start = ((), (), s32[]{:S(2)}) async-start(), calls=%async_computation.7 | async-start | bytes 1671168 | tf_op jit(solution)/shard_map/all_gather | solution.py:45
  13.1 22.3 %all-to-all-start = ((bf16[32,1,12]{2,1,0:T(2,128)(2,1)}), bf16[32,1,12]{2,1,0:T(2,128)(2,1)S(1)}, u32[]{:S(2)}, u32[]{:S(2)}) async-start(bf16[32,1,12]{2,1,0:T(2,128)(2,1)} %all_to_all.25), calls=%async_computation | async-start | bytes 32768 | tf_op jit(solution)/shard_map/all_to_all | solution.py:78
  29.0 10.5 %copy-start.11 = (s32[1,32,384]{2,1,0:T(8,128)S(1)}, s32[1,32,384]{2,1,0:T(8,128)}, u32[]{:S(2)}) copy-start(s32[1,32,384]{2,1,0:T(8,128)} %param.21) | copy-start | bytes 147460
  29.0 10.5 %copy-start.13 = (bf16[6,4,1]{0,1,2:T(4,128)(2,1)S(1)}, bf16[6,4,1]{0,1,2:T(4,128)(2,1)}, u32[]{:S(2)}) copy-start(bf16[6,4,1]{0,1,2:T(4,128)(2,1)} %constant.70) | copy-start | bytes 148
  29.0 10.8 %copy-start.6 = (bf16[1,128,384]{2,1,0:T(8,128)(2,1)S(1)}, bf16[1,128,384]{2,1,0:T(8,128)(2,1)}, u32[]{:S(2)}) copy-start(bf16[1,128,384]{2,1,0:T(8,128)(2,1)} %param.18) | copy-start | bytes 294916
  35.4 53.4 %all-to-all-start.2 = ((bf16[32,12,2048]{2,1,0:T(8,128)(2,1)}), bf16[32,12,2048]{2,1,0:T(8,128)(2,1)S(1)}, u32[]{:S(2)}, u32[]{:S(2)}) async-start(bf16[32,12,2048]{2,1,0:T(8,128)(2,1)} %reshape.97), calls=%async_computation.2 | async-start | bytes 4194304 | tf_op jit(solution)/shard_map/all_to_all | solution.py:64
  39.4 112.1 %all-gather.6.cloned.1.call-start = ((), (), s32[]{:S(2)}) async-start(), calls=%async_computation.6 | async-start | bytes 1671168 | tf_op jit(solution)/shard_map/all_gather | solution.py:46
  46.9 48.2 %copy-start.12 = (s32[1,96,128]{2,1,0:T(8,128)S(1)}, s32[1,96,128]{2,1,0:T(8,128)}, u32[]{:S(2)}) copy-start(s32[1,96,128]{2,1,0:T(8,128)} %param.22) | copy-start | bytes 147460
  46.9 48.5 %copy-start.10 = (bf16[1,384,128]{2,1,0:T(8,128)(2,1)S(1)}, bf16[1,384,128]{2,1,0:T(8,128)(2,1)}, u32[]{:S(2)}) copy-start(bf16[1,384,128]{2,1,0:T(8,128)(2,1)} %param.19) | copy-start | bytes 294916
  88.8 55.6 %all-to-all-start.1 = ((bf16[32,12,2048]{2,1,0:T(8,128)(2,1)}), bf16[32,12,2048]{2,1,0:T(8,128)(2,1)}, u32[]{:S(2)}, u32[]{:S(2)}) async-start(bf16[32,12,2048]{2,1,0:T(8,128)(2,1)} %reshape.95), calls=%async_computation.1 | async-start | bytes 4194304 | tf_op jit(solution)/shard_map/all_to_all | solution.py:71
  95.1 59.7 %all-gather.4.cloned.1.call-start = ((), (), s32[]{:S(2)}) async-start(), calls=%async_computation.5 | async-start | bytes 1671168 | tf_op jit(solution)/shard_map/all_gather | solution.py:47
  97.6 50.7 %copy-start.2 = (bf16[384,2048]{1,0:T(8,128)(2,1)S(1)}, bf16[384,2048]{1,0:T(8,128)(2,1)}, u32[]{:S(2)}) copy-start(bf16[384,2048]{1,0:T(8,128)(2,1)} %reshape.98) | copy-start | bytes 4718596
  154.7 11.0 %copy-start.15 = (bf16[384,2048]{1,0:T(8,128)(2,1)S(1)}, bf16[384,2048]{1,0:T(8,128)(2,1)}, u32[]{:S(2)}) copy-start(bf16[384,2048]{1,0:T(8,128)(2,1)} %all-gather.4.cloned.1.call-done) | copy-start | bytes 4718596
  159.4 14.9 %all-to-all-start.4 = ((bf16[32,1,12]{2,1,0:T(2,128)(2,1)}), bf16[32,1,12]{2,1,0:T(2,128)(2,1)S(1)}, u32[]{:S(2)}, u32[]{:S(2)}) async-start(bf16[32,1,12]{2,1,0:T(2,128)(2,1)} %convert_element_type.162), calls=%async_computation.4 | async-start | bytes 32768 | tf_op jit(solution)/shard_map/all_to_all | solution.py:116
  165.8 3.5 %copy-start.1 = (bf16[2048,384]{1,0:T(8,128)(2,1)S(1)}, bf16[2048,384]{1,0:T(8,128)(2,1)}, u32[]{:S(2)}) copy-start(bf16[2048,384]{1,0:T(8,128)(2,1)} %all-gather.8.cloned.1.call-done) | copy-start | bytes 4718596
  169.3 1.6 copy-start.4
  174.3 143.4 %all-to-all-start.3 = ((bf16[32,12,2048]{2,1,0:T(8,128)(2,1)}), bf16[32,12,2048]{2,1,0:T(8,128)(2,1)S(1)}, u32[]{:S(2)}, u32[]{:S(2)}) async-start(bf16[32,12,2048]{2,1,0:T(8,128)(2,1)} %reshape.101), calls=%async_computation.3 | async-start | bytes 4194304 | tf_op jit(solution)/shard_map/all_to_all | solution.py:109
  182.7 133.3 %all-reduce.3.cloned.1.call-start = ((), (), s32[]{:S(2)}) async-start(), calls=%async_computation.8 | async-start | bytes 6291456 | tf_op jit(solution)/shard_map/psum | solution.py:137
  182.9 3.9 %copy-start.3 = (bf16[384,2048]{1,0:T(8,128)(2,1)S(1)}, bf16[384,2048]{1,0:T(8,128)(2,1)}, u32[]{:S(2)}) copy-start(bf16[384,2048]{1,0:T(8,128)(2,1)} %reshape.98) | copy-start | bytes 4718596
  182.9 3.9 %copy-start.8 = (bf16[384,384]{1,0:T(8,128)(2,1)S(1)}, bf16[384,384]{1,0:T(8,128)(2,1)}, u32[]{:S(2)}) copy-start(bf16[384,384]{1,0:T(8,128)(2,1)} %copy-done.7) | copy-start | bytes 884740
  189.2 126.7 %copy-start.5 = (bf16[1,128,384]{2,1,0:T(8,128)(2,1)S(1)}, bf16[1,128,384]{2,1,0:T(8,128)(2,1)}, u32[]{:S(2)}) copy-start(bf16[1,128,384]{2,1,0:T(8,128)(2,1)} %param.17) | copy-start | bytes 294916
  (2 other events, 2.1 us)
Sparse Core Ops, SparseCore 0:
  10.7 47.3 all-gather.7
  60.8 40.4 all-gather.5
  103.9 40.7 all-gather.3
  189.3 126.5 all-reduce.2
where the time goes:
time: 329 us; the launch traced here: 328 us
  waiting for transfers between devices  222 us (67%)
  starting transfers between devices  39 us (12%)
  matrix products  29.9 us (9%)
  local copies, waits for them, and re-layouts  17.2 us (5%)
  between operations  14.1 us (4%)
  other arithmetic  6.07 us (2%)
    psum x1, waiting for transfers between devices, per_device(): lax.psum(part_gate.astype(jnp.bfloat16), 'dp').astype(jnp.float32)  126 us
    all_to_all x1, waiting for transfers between devices, per_device(): lax.all_to_all(send_grads.reshape(expert_count, capacity, model_width), '...  46.8 us
    all_to_all x1, waiting for transfers between devices, per_device(): lax.all_to_all(send_rows.reshape(expert_count, capacity, model_width), 'e...  41.9 us
    all_to_all x1, starting transfers between devices, per_device(): lax.all_to_all(send_probs.reshape(expert_count, capacity), 'expert', spli...  13.7 us
    all_to_all x1, starting transfers between devices, per_device(): lax.all_to_all(slot_grad.reshape(expert_count, capacity, model_width), 'e...  8.35 us
  transfers between devices with their start and end apart: 9, of which 5 were waited for; matrix products, arithmetic and copies ran while one was open for 12% of the time, Pallas kernels for 0%

commit v1 on v0

v1 whole, which is shorter than its diff:
```python
import functools

import jax
import jax.numpy as jnp
from jax import lax
from jax.experimental import pallas as pl
from jax.experimental.pallas import tpu as pltpu
from jax.sharding import PartitionSpec as P

decay_rate = 24.0
main_slots = 8
tail_slots = 4
lane = 128
large = 56
weight_chunks = 4
f32 = jnp.float32
bf16 = jnp.bfloat16
vmem = pl.BlockSpec(memory_space=pltpu.VMEM)
near = pl.BlockSpec(memory_space=pltpu.VMEM)
hbm = pl.BlockSpec(memory_space=pltpu.HBM)
pins = {id(near): pltpu.VMEM, id(hbm): pltpu.HBM}
smem = pl.BlockSpec(memory_space=pltpu.SMEM)


def iota(shape, dim):
    return lax.broadcasted_iota(jnp.int32, shape, dim)


def dot(a, b, dims=((1,), (0,))):
    return lax.dot_general(a, b, (dims, ((), ())), preferred_element_type=f32)


def call(kernel, out_shape, in_specs, out_specs, cost, scratch=(), name=None, mib=12):
    flops, moved = cost

    def run(*args):
        pinned = [
            pltpu.with_memory_space_constraint(x, pins[id(spec)]) if id(spec) in pins else x
            for x, spec in zip(args, in_specs)
        ]
        return kernel_call(*pinned)

    if isinstance(out_specs, tuple):
        out_shape = tuple(
            pins[id(spec)](s.shape, s.dtype) if id(spec) in pins else s
            for s, spec in zip(out_shape, out_specs)
        )
    kernel_call = pl.pallas_call(
        kernel,
        out_shape=out_shape,
        in_specs=in_specs,
        out_specs=out_specs,
        scratch_shapes=scratch,
        compiler_params=pltpu.CompilerParams(vmem_limit_bytes=mib * 1024 * 1024),
        cost_estimate=pl.CostEstimate(flops=flops, bytes_accessed=moved, transcendentals=0),
        name=name,
    )
    return run


def place_kernel(ids_ref, probs_ref, tokens_hbm, grads_hbm, out_hbm, target_ref, tokens, grads, out, sems):
    count, width = tokens.shape
    half = width // 2
    slot_rows = out.shape[0]
    experts = slot_rows // main_slots
    loads = [
        pltpu.make_async_copy(tokens_hbm, tokens, sems.at[0]),
        pltpu.make_async_copy(grads_hbm, grads, sems.at[1]),
    ]
    for load in loads:
        load.start()
    ids = [ids_ref[k : k + 1, :] for k in range(2)]
    named = [(iota((experts, count), 0) == ids[k]).astype(f32) for k in range(2)]
    before = (iota((count, count), 0) < iota((count, count), 1)).astype(bf16)
    earlier = dot((named[0] + named[1]).astype(bf16), before)
    row = iota((slot_rows, count), 0)
    main_hit, tail_hit, targets = [], [], []
    for k in range(2):
        slot = jnp.sum(earlier * named[k], axis=0, keepdims=True).astype(jnp.int32)
        main = jnp.where(slot < main_slots, ids[k] * main_slots + slot, -100)
        tail = jnp.where(slot < main_slots, -100, ids[k] * main_slots + slot - main_slots)
        targets += [main, tail]
        main_hit.append(row == main)
        tail_hit.append((row == tail, row == tail + tail_slots))
    probs = [probs_ref[k : k + 1, :].astype(f32) for k in range(2)]
    target_ref[...] = jnp.concatenate([t.astype(f32) for t in targets] + probs + probs, axis=0)

    def placing(hit, scale):
        return (jnp.where(hit[0], scale[0], 0.0) + jnp.where(hit[1], scale[1], 0.0)).astype(bf16)

    stores = []

    def store(start, size):
        span = (slice(None), pl.ds(start, size))
        sem = sems.at[2 + len(stores)]
        stores.append(pltpu.make_async_copy(out.at[span], out_hbm.at[span], sem))
        stores[-1].start()

    for at, (source, scale) in enumerate(((tokens, (1.0, 1.0)), (grads, probs))):
        base = at * (width + half)
        main = placing(main_hit, scale)
        tail = jnp.concatenate(
            [placing([tail_hit[k][side] for k in range(2)], scale) for side in range(2)], axis=1
        )
        loads[at].wait()
        out[:, base : base + width] = dot(main, source[...]).astype(bf16)
        store(base, width)
        halves = jnp.concatenate([source[:, :half], source[:, half:]], axis=0)
        out[:, base + width : base + width + half] = dot(tail, halves).astype(bf16)
        store(base + width, half)
    for copy in stores:
        copy.wait()


def kept(pattern_ref):
    groups = pattern_ref.shape[0]
    rows = groups * 4
    spread = (iota((rows, groups), 0) // 4 == iota((rows, groups), 1)).astype(bf16)
    p = dot(spread, pattern_ref[...].astype(f32).astype(bf16))
    j = iota(p.shape, 0) % 4
    one = (p == 0.0) | (p == 3.0) | (p == 4.0)
    two = (p == 1.0) | (p == 3.0) | (p == 5.0)
    three = (p == 2.0) | (p >= 4.0)
    keep = ((j == 0) & (p <= 2.0)) | ((j == 1) & one) | ((j == 2) & two) | ((j == 3) & three)
    return keep


def mask_kernel(
    gate_ref, up_ref, down_ref, gate_mask_ref, up_mask_ref, down_mask_ref, out_ref, decay_ref
):
    hidden = gate_ref.shape[1]
    for at, (weight, mask) in enumerate(((gate_ref, gate_mask_ref), (up_ref, up_mask_ref))):
        span = slice(at * hidden, (at + 1) * hidden)
        keep, dense = kept(mask), weight[...].astype(f32)
        out_ref[:, span] = jnp.where(keep, dense, 0.0).astype(bf16)
        decay_ref[:, span] = jnp.where(keep, 0.0, decay_rate * dense)
    masked = jnp.where(kept(down_mask_ref), down_ref[...].astype(f32), 0.0)
    out_ref[:, 2 * hidden :] = masked.T.astype(bf16)


def tail_sides(rows):
    wide = rows * main_slots // tail_slots
    r = iota((rows, wide), 0)
    low = r // tail_slots * main_slots + r % tail_slots
    c = iota((rows, wide), 1)
    return (c == low).astype(bf16), (c == low + tail_slots).astype(bf16)


def tail_sides_t(rows):
    wide = rows * main_slots // tail_slots
    r = iota((wide, rows), 1)
    low = r // tail_slots * main_slots + r % tail_slots
    c = iota((wide, rows), 0)
    return (c == low).astype(bf16), (c == low + tail_slots).astype(bf16)


def assemble_kernel(order, place_ref, target_ref, *refs):
    pieces = 2 * len(order)
    piece_refs = refs[:pieces]
    weight_hbm, left_ref, right_ref, weight, sems = refs[pieces:]
    depth = piece_refs[0].shape[0]
    y, core = place_ref[0], place_ref[1]
    copies = []
    for k in range(pieces):
        origin = lax.rem(y + (len(order) - order[k % len(order)]), len(order))
        offset = (2 * origin + (core if k < len(order) else 1 - core)) * depth
        to = weight.at[pl.ds(pl.multiple_of(offset, depth), depth)]
        copies.append(pltpu.make_async_copy(piece_refs[k], to, sems.at[k]))
        copies[-1].start()
    count = target_ref.shape[1]
    slot_rows = left_ref.shape[1] // 2
    row = iota((slot_rows, count), 0).astype(f32)
    main0, tail0, main1, tail1 = [target_ref[k : k + 1, :] for k in range(4)]
    main = ((row == main0) | (row == main1)).astype(f32).T.astype(bf16)
    low = ((row == tail0) | (row == tail1)).astype(f32).T.astype(bf16)
    high = ((row == tail0 + tail_slots) | (row == tail1 + tail_slots)).astype(f32).T.astype(bf16)
    left_ref[:, :slot_rows] = main
    left_ref[:, slot_rows:] = low
    right_ref[:, :slot_rows] = main
    right_ref[:, slot_rows:] = high
    for copy in copies:
        copy.wait()
    store = pltpu.make_async_copy(weight, weight_hbm, sems.at[pieces])
    store.start()
    store.wait()


def weight_grads(place_ref, delta_t_ref, rows_ref, out, own, after):
    steps = out.shape[0]
    y, core = place_ref[0], place_ref[1]
    side = (core if own else 1 - core) * lane

    def columns(d):
        at = lax.rem(y + d, steps) * 2 * lane + side
        return rows_ref[:, pl.ds(pl.multiple_of(at, lane), lane)]

    for d in range(0, steps, 2):
        part = dot(delta_t_ref[...], jnp.concatenate([columns(d), columns(d + 1)], axis=1))
        out[d] = part[:, :lane].astype(bf16)
        out[d + 1] = part[:, lane:].astype(bf16)
        after(d)


def delta_kernel(
    place_ref,
    x_ref,
    weight_hbm,
    delta_ref,
    prob_ref,
    delta_t_ref,
    rows,
    weight,
    other_hbm,
    down,
    cotan,
    other,
    sems,
    load_sems,
):
    width, hidden = down.shape
    half = width // 2
    depth = width // weight_chunks
    spans = [slice(k * depth, (k + 1) * depth) for k in range(weight_chunks)]
    loads = [
        pltpu.make_async_copy(weight_hbm.at[span, pl.ds(0, 2 * hidden)], weight.at[span], load_sems.at[k])
        for k, span in enumerate(spans)
    ]
    loads.append(
        pltpu.make_async_copy(
            weight_hbm.at[:, pl.ds(2 * hidden, hidden)], down, load_sems.at[weight_chunks]
        )
    )
    for load in loads:
        load.start()
    main_rows = x_ref.shape[0]
    tail_rows = main_rows * tail_slots // main_slots
    low, high = tail_sides(tail_rows)
    for at, target in enumerate((rows, cotan)):
        base = at * (width + half)
        target[:main_rows, :] = x_ref[:, base : base + width]
        halves = x_ref[:, base + width : base + width + half]
        target[main_rows:, :half] = dot(low, halves).astype(bf16)
        target[main_rows:, half:] = dot(high, halves).astype(bf16)
    pre = 0.0
    for load, span in zip(loads, spans):
        load.wait()
        pre = pre + dot(rows[:, span], weight[span, :])
    loads[-1].wait()
    grad = dot(cotan[...], down[...])
    gate_pre, up_pre = pre[:, :hidden], pre[:, hidden:]
    sig = jax.nn.sigmoid(gate_pre)
    silu = gate_pre * sig
    act = (silu * up_pre).astype(bf16)
    prob = jnp.sum(act.astype(f32) * grad, axis=1, keepdims=True)
    prob_ref[...] = jnp.broadcast_to(prob, prob_ref.shape).astype(bf16)
    gate_delta = (grad * up_pre * sig * (1.0 + gate_pre * (1.0 - sig))).astype(bf16)
    up_delta = (grad * silu).astype(bf16)
    delta_ref[:, :hidden] = gate_delta
    delta_ref[:, hidden:] = up_delta
    delta_t_ref[:hidden, :] = gate_delta.T
    delta_t_ref[hidden:, :] = up_delta.T
    stores = []

    def after(d):
        span = pl.ds(d, 2)
        stores.append(pltpu.make_async_copy(other.at[span], other_hbm.at[span], sems.at[d // 2]))
        stores[-1].start()

    weight_grads(place_ref, delta_t_ref, rows, other, False, after)
    for copy in stores:
        copy.wait()


def slot_grad_kernel(
    place_ref, delta_ref, prob_ref, delta_t_ref, rows_ref, weight_ref, out_hbm, mine_ref, out, sems
):
    width = weight_ref.shape[0]
    half = width // 2
    main_rows = out.shape[0]
    tail_rows = delta_ref.shape[0] - main_rows
    stores = []

    def store(start, size):
        span = (slice(None), pl.ds(start, size))
        sem = sems.at[len(stores)]
        stores.append(pltpu.make_async_copy(out.at[span], out_hbm.at[span], sem))
        stores[-1].start()

    low_t, high_t = tail_sides_t(tail_rows)
    tails = []
    for at in range(2):
        span = slice(at * half, (at + 1) * half)
        back = dot(delta_ref[...], weight_ref[span, :], ((1,), (1,))).astype(bf16)
        out[:, span] = back[:main_rows]
        store(at * half, half)
        tails.append(back[main_rows:])
    tail = dot(low_t, tails[0]) + dot(high_t, tails[1])
    out[:, width : width + half] = tail.astype(bf16)
    at_lane = iota((main_rows, lane), 1)
    late = dot(low_t, prob_ref[main_rows:, :])
    probs = jnp.where(at_lane == 1, late, prob_ref[:main_rows, :].astype(f32))
    out[:, width + half :] = probs.astype(bf16)
    store(width, half + lane)
    weight_grads(place_ref, delta_t_ref, rows_ref, mine_ref, True, lambda d: None)
    for copy in stores:
        copy.wait()


def pair_sum_kernel(mine_ref, got_ref, *refs):
    steps = mine_ref.shape[0]
    outs, sums, sems = refs[:steps], refs[steps], refs[steps + 1]
    stores = []
    for d, out in enumerate(outs):
        sums[d] = (mine_ref[d].astype(f32) + got_ref[d].astype(f32)).astype(bf16)
        stores.append(pltpu.make_async_copy(sums.at[d], out, sems.at[d]))
        stores[-1].start()
    for copy in stores:
        copy.wait()


def finish_weights_kernel(decay_ref, *refs):
    gate_out, up_out = refs[-2:]
    hidden = gate_out.shape[1]
    total = refs[0][...].astype(f32)
    for ref in refs[1:-2]:
        total = total + ref[...].astype(f32)
    total = total.T + decay_ref[...]
    gate_out[...] = total[:, :hidden]
    up_out[...] = total[:, hidden:]


def finish_tokens_kernel(target_ref, left_ref, right_ref, back_ref, grad_ref, prob_ref):
    width = grad_ref.shape[1]
    half = width // 2
    slot_rows = back_ref.shape[0]
    tail = back_ref[:, width : width + half]
    for at, place in enumerate((left_ref, right_ref)):
        span = slice(at * half, (at + 1) * half)
        stacked = jnp.concatenate([back_ref[:, span], tail], axis=0)
        grad_ref[:, span] = dot(place[...], stacked).astype(bf16)
    returned = back_ref[:, width + half :].astype(f32)
    row = iota((slot_rows, target_ref.shape[1]), 0).astype(f32)
    for k in range(2):
        main, late = target_ref[2 * k : 2 * k + 1, :], target_ref[2 * k + 1 : 2 * k + 2, :]
        picked = jnp.where(row == main, returned[:, 0:1], 0.0)
        picked = picked + jnp.where(row == late, returned[:, 1:2], 0.0)
        total = jnp.sum(picked, axis=0, keepdims=True)
        prob_ref[k : k + 1, :] = (total / target_ref[4 + k : 5 + k, :]).astype(bf16)


def per_device(
    tokens,
    out_grad,
    expert_ids,
    route_probs,
    gate_weight,
    up_weight,
    down_weight,
    gate_mask,
    up_mask,
    down_mask,
):
    count, width = tokens.shape
    half = width // 2
    hidden = gate_weight.shape[2]
    experts = lax.axis_size("expert")
    dp = lax.axis_size("dp")
    ny = dp // 2
    slot_rows = experts * main_slots
    all_rows = experts * (main_slots + tail_slots)
    me = lax.axis_index("dp")
    here = jnp.stack([lax.shift_right_logical(me, 1), lax.bitwise_and(me, 1)])
    sds = jax.ShapeDtypeStruct
    ids, probs = expert_ids.T, route_probs.T

    sent, targets = call(
        place_kernel,
        (sds((slot_rows, 3 * width), bf16), sds((8, count), f32)),
        [vmem, vmem, hbm, hbm],
        (hbm, vmem),
        (slot_rows * count * width * 10, 5 * slot_rows * width * 2),
        scratch=(
            pltpu.VMEM((count, width), bf16),
            pltpu.VMEM((count, width), bf16),
            pltpu.VMEM((slot_rows, 3 * width), bf16),
            pltpu.SemaphoreType.DMA((6,)),
        ),
        name="place",
        mib=large,
    )(ids, probs, tokens, out_grad)

    def exchange(x):
        blocks = x.reshape(experts, main_slots, x.shape[1])
        moved = lax.all_to_all(blocks, "expert", split_axis=0, concat_axis=0, tiled=True)
        return moved.reshape(x.shape)

    arrived = exchange(sent)

    piece, decay = call(
        mask_kernel,
        (sds((width // dp, 3 * hidden), bf16), sds((width // dp, 2 * hidden), f32)),
        [vmem] * 6,
        (vmem, vmem),
        (width * hidden * 100, 6 * width // dp * hidden),
        name="mask",
        mib=large,
    )(gate_weight[0], up_weight[0], down_weight[0], gate_mask[0], up_mask[0], down_mask[0])

    def along_y(x, d):
        moves = [(2 * a + c, 2 * ((a + d) % ny) + c) for a in range(ny) for c in range(2)]
        return lax.ppermute(x, "dp", moves)

    def across(x):
        return lax.ppermute(x, "dp", [(i, i ^ 1) for i in range(dp)])

    forward, backward = [piece], [piece]
    for _ in range(ny // 2):
        forward.append(along_y(forward[-1], 1))
        backward.append(along_y(backward[-1], ny - 1))
    held = [(0, piece)] + [(d, forward[d]) for d in range(1, ny // 2 + 1)]
    held += [(ny - d, backward[d]) for d in range(1, ny // 2)]
    other = [across(x) for _, x in held]
    weights, place_left, place_right = call(
        functools.partial(assemble_kernel, [d for d, _ in held]),
        (sds((width, 3 * hidden), bf16),) + (sds((count, 2 * slot_rows), bf16),) * 2,
        [smem, vmem] + [hbm] * dp,
        (hbm, vmem, vmem),
        (count * slot_rows * 10, 6 * width * hidden),
        scratch=(
            pltpu.VMEM((width, 3 * hidden), bf16),
            pltpu.SemaphoreType.DMA((dp + 1,)),
        ),
        name="assemble",
    )(here, targets, *[x for _, x in held], *other)

    block = (2 * hidden, lane)
    delta, slot_probs, delta_t, rows, gate_up, theirs = call(
        delta_kernel,
        (
            sds((all_rows, 2 * hidden), bf16),
            sds((all_rows, lane), bf16),
            sds((2 * hidden, all_rows), bf16),
            sds((all_rows, width), bf16),
            sds((width, 2 * hidden), bf16),
            sds((ny, *block), bf16),
        ),
        [smem, vmem, hbm],
        (near,) * 5 + (hbm,),
        (all_rows * width * hidden * 8, 12 * slot_rows * width),
        scratch=(
            pltpu.VMEM((width, hidden), bf16),
            pltpu.VMEM((all_rows, width), bf16),
            pltpu.VMEM((ny, *block), bf16),
            pltpu.SemaphoreType.DMA((ny // 2,)),
            pltpu.SemaphoreType.DMA((weight_chunks + 1,)),
        ),
        name="delta",
        mib=24,
    )(here, arrived, weights)
    got = across(theirs)
    returned, mine = call(
        slot_grad_kernel,
        (sds((slot_rows, width + half + lane), bf16), sds((ny, *block), bf16)),
        [smem] + [near] * 5,
        (hbm, near),
        (all_rows * width * hidden * 6, 12 * slot_rows * width),
        scratch=(
            pltpu.VMEM((slot_rows, width + half + lane), bf16),
            pltpu.SemaphoreType.DMA((3,)),
        ),
        name="slot_grad",
        mib=24,
    )(here, delta, slot_probs, delta_t, rows, gate_up)
    sums = call(
        pair_sum_kernel,
        (sds(block, bf16),) * ny,
        [near, vmem],
        (hbm,) * ny,
        (width * hidden * 2, 12 * width * hidden),
        scratch=(pltpu.VMEM((ny, *block), bf16), pltpu.SemaphoreType.DMA((ny,))),
        name="pair_sum",
    )(mine, got)
    returned, *sums = lax.optimization_barrier((returned, *sums))
    back = exchange(returned)
    far_first = sorted(range(1, ny), key=lambda d: -min(d, ny - d))
    terms = [sums[0]] + [along_y(sums[d], d) for d in far_first]
    gate_grad, up_grad = call(
        finish_weights_kernel,
        (sds((width // dp, hidden), f32),) * 2,
        [vmem] * (1 + ny),
        (vmem, vmem),
        (width * hidden * 2, 4 * width * hidden),
        name="finish_weights",
    )(decay, *terms)
    token_grad, prob_grad = call(
        finish_tokens_kernel,
        (sds((count, width), bf16), sds((2, count), bf16)),
        [vmem] * 4,
        (vmem, vmem),
        (count * slot_rows * width * 4, 6 * slot_rows * width),
        name="finish_tokens",
        mib=16,
    )(targets, place_left, place_right, back)
    return token_grad, prob_grad.T, gate_grad[None], up_grad[None]


def solution(mesh):
    placed = (
        P(("dp", "expert"), None),
        P(("dp", "expert"), None),
        P(("dp", "expert"), None),
        P(("dp", "expert"), None),
        P("expert", "dp", None),
        P("expert", "dp", None),
        P("expert", None, "dp"),
        P("expert", "dp", None),
        P("expert", "dp", None),
        P("expert", None, "dp"),
    )
    return jax.shard_map(
        per_device,
        mesh=mesh,
        in_specs=placed,
        out_specs=(
            P(("dp", "expert"), None),
            P(("dp", "expert"), None),
            P("expert", "dp", None),
            P("expert", "dp", None),
        ),
        check_vma=False,
    )
```

time: 329 us -> 160 us (0.49)
  waiting for transfers between devices: 222 us -> 36 us
  starting transfers between devices: 39 us -> 95.3 us
  matrix products: 29.9 us -> 0 us
  Pallas kernels: 0 us -> 27 us
  local copies, waits for them, and re-layouts: 17.2 us -> 0.04 us
  between operations: 14.1 us -> 1.07 us
  other arithmetic: 6.07 us -> 0.08 us
    psum x1 -> x0, waiting for transfers between devices: 126 us -> none  [per_device(): lax.psum(part_gate.astype(jnp.bfloat16), 'dp').astype(jnp.float32)]
    all_to_all x5 -> x2, waiting for transfers between devices: 96 us -> 9.66 us  [exchange(): lax.all_to_all(blocks, 'expert', split_axis=0, concat_axis=0, tiled=True)]
    ppermute x0 -> x23, starting transfers between devices: none -> 75.9 us  [the longest x14 49.5 us: along_y(): return lax.ppermute(x, 'dp', moves)]
    dot_general x16 -> x0, matrix products: 29.9 us -> none  [the longest x1 3.92 us: per_device(): jnp.einsum('rd,rh->dh', inputs, up_delta, preferred_element_type=jnp.floa...]
    pallas_call x0 -> x8, Pallas kernels: none -> 27 us  [run(): return kernel_call(*pinned)]
    ppermute x0 -> x23, waiting for transfers between devices: none -> 26.4 us  [the longest x14 24.9 us: along_y(): return lax.ppermute(x, 'dp', moves)]
    all_to_all x5 -> x2, starting transfers between devices: 38.7 us -> 19.4 us  [exchange(): lax.all_to_all(blocks, 'expert', split_axis=0, concat_axis=0, tiled=True)]
    reshape x8 -> x0, local copies, waits for them, and re-layouts: 9.61 us -> none  [the longest x1 3.6 us: per_device(): send_grads.reshape(expert_count, capacity, model_width)]
  transfers between devices with their start and end apart: 9 -> 25, of which waited for: 5 -> 10; matrix products, arithmetic and copies ran while one was open for 12% -> 0% of each run, Pallas kernels for 0% -> 8%
where the time goes in v1:
time: 160 us; the launch traced here: 159 us
  starting transfers between devices  95.3 us (60%)
  waiting for transfers between devices  36 us (22%)
  Pallas kernels  27 us (17%)
    ppermute x14, starting transfers between devices, along_y(): return lax.ppermute(x, 'dp', moves)  49.5 us
    pallas_call x8, Pallas kernels, run(): return kernel_call(*pinned)  27 us
    ppermute x9, starting transfers between devices, across(): return lax.ppermute(x, 'dp', [(i, i ^ 1) for i in range(dp)])  26.4 us
    ppermute x14, waiting for transfers between devices, along_y(): return lax.ppermute(x, 'dp', moves)  24.9 us
    all_to_all x2, starting transfers between devices, exchange(): lax.all_to_all(blocks, 'expert', split_axis=0, concat_axis=0, tiled=True)  19.4 us
    all_to_all x2, waiting for transfers between devices, exchange(): lax.all_to_all(blocks, 'expert', split_axis=0, concat_axis=0, tiled=True)  9.66 us
  transfers between devices with their start and end apart: 25, of which 10 were waited for; matrix products, arithmetic and copies ran while one was open for 0% of the time, Pallas kernels for 8%

profile of v1, /device:TPU:1, one launch (start us, length us, event | category | flops | bytes accessed | tf_op | source)
XLA Modules:
  0.0 159.5 jit_solution(13387326323298955550)
XLA Ops:
  0.6 4.5 %place.1 = (bf16[256,6144]{1,0:T(8,128)(2,1)}, f32[8,128]{1,0:T(8,128)}) custom-call(s32[2,128]{1,0:T(2,128)} %bitcast.29, bf16[2,128]{1,0:T(2,128)(2,1)} %bitcast.30, bf16[128,2048]{1,0:T(8,128)(2,1)} %tokens_hbm.1, bf16[128,2048]{1,0:T(8,128)(2,1)} %grads_hbm.1), custom_call_target="tpu_custom_call" | custom-call | flops 671088640 | bytes 5242880 | tf_op jit(solution)/shard_map/place/pallas_call | solution.py:41
  5.2 13.7 %all-to-all-start = ((bf16[32,8,6144]{2,1,0:T(8,128)(2,1)}), bf16[32,8,6144]{2,1,0:T(8,128)(2,1)S(1)}, u32[]{:S(2)}, u32[]{:S(2)}) async-start(bf16[32,8,6144]{2,1,0:T(8,128)(2,1)} %bitcast.19), calls=%async_computation | async-start | bytes 6291456 | tf_op jit(solution)/shard_map/all_to_all | solution.py:394
  18.9 3.0 %mask.1 = (bf16[128,1152]{1,0:T(8,128)(2,1)}, f32[128,768]{1,0:T(8,128)}) custom-call(bf16[128,384]{1,0:T(8,128)(2,1)} %bitcast.21, bf16[128,384]{1,0:T(8,128)(2,1)} %bitcast.22, bf16[384,128]{1,0:T(8,128)(2,1)} %bitcast.23, s32[32,384]{1,0:T(8,128)} %bitcast.24, s32[32,384]{1,0:T(8,128)} %bitcast.25, s32[96,128]{1,0:T(8,128)} %bitcast.26), custom_call_target="tpu_custom_call" | custom-call | flops 78643200 | bytes 294912 | tf_op jit(solution)/shard_map/mask/pallas_call | solution.py:41
  21.9 3.2 %collective-permute-start = (bf16[128,1152]{1,0:T(8,128)(2,1)}, bf16[128,1152]{1,0:T(8,128)(2,1)S(1)}, u32[]{:S(2)}, u32[]{:S(2)}) collective-permute-start(bf16[128,1152]{1,0:T(8,128)(2,1)} %get-tuple-element.41.refs_0_), channel_id=1, source_target_pairs={{0,64},{32,96},{64,128},{96,160},{128,192},{160,224},{192,256},{22... | collective-permute-start | bytes 884744 | tf_op jit(solution)/shard_map/ppermute | solution.py:411
  25.1 3.8 %collective-permute-start.4 = (bf16[128,1152]{1,0:T(8,128)(2,1)}, bf16[128,1152]{1,0:T(8,128)(2,1)S(1)}, u32[]{:S(2)}, u32[]{:S(2)}) collective-permute-start(bf16[128,1152]{1,0:T(8,128)(2,1)} %get-tuple-element.41.refs_0_), channel_id=1, source_target_pairs={{0,448},{32,480},{64,0},{96,32},{128,64},{160,96},{192,128},{224,1... | collective-permute-start | bytes 884744 | tf_op jit(solution)/shard_map/ppermute | solution.py:411
  28.9 4.7 %collective-permute-done.refs_1_ = bf16[128,1152]{1,0:T(8,128)(2,1)S(1)} collective-permute-done((bf16[128,1152]{1,0:T(8,128)(2,1)}, bf16[128,1152]{1,0:T(8,128)(2,1)S(1)}, u32[]{:S(2)}, u32[]{:S(2)}) %collective-permute-start) | collective-permute-done | bytes 294944 | tf_op jit(solution)/shard_map/ppermute | solution.py:411
  35.6 4.6 %collective-permute-start.5 = (bf16[128,1152]{1,0:T(8,128)(2,1)S(1)}, bf16[128,1152]{1,0:T(8,128)(2,1)}, u32[]{:S(2)}, u32[]{:S(2)}) collective-permute-start(bf16[128,1152]{1,0:T(8,128)(2,1)S(1)} %collective-permute-done.4.refs_5_), channel_id=1, source_target_pairs={{0,448},{32,480},{64,0},{96,32},{128,64},{160,96},{192,128},{224,1... | collective-permute-start | bytes 884744 | tf_op jit(solution)/shard_map/ppermute | solution.py:411
  40.1 3.6 %collective-permute-done.1.refs_2_ = bf16[128,1152]{1,0:T(8,128)(2,1)} collective-permute-done((bf16[128,1152]{1,0:T(8,128)(2,1)S(1)}, bf16[128,1152]{1,0:T(8,128)(2,1)}, u32[]{:S(2)}, u32[]{:S(2)}) %collective-permute-start.1) | collective-permute-done | bytes 294944 | tf_op jit(solution)/shard_map/ppermute | solution.py:411
  45.7 4.4 %collective-permute-start.7 = (bf16[128,1152]{1,0:T(8,128)(2,1)}, bf16[128,1152]{1,0:T(8,128)(2,1)S(1)}, u32[]{:S(2)}, u32[]{:S(2)}) collective-permute-start(bf16[128,1152]{1,0:T(8,128)(2,1)} %get-tuple-element.41.refs_0_), channel_id=1, source_target_pairs={{0,32},{32,0},{64,96},{96,64},{128,160},{160,128},{192,224},{224,1... | collective-permute-start | bytes 884744 | tf_op jit(solution)/shard_map/ppermute | solution.py:414
  54.4 4.9 %collective-permute-start.6 = (bf16[128,1152]{1,0:T(8,128)(2,1)}, bf16[128,1152]{1,0:T(8,128)(2,1)}, u32[]{:S(2)}, u32[]{:S(2)}) collective-permute-start(bf16[128,1152]{1,0:T(8,128)(2,1)} %collective-permute-done.5.refs_6_), channel_id=1, source_target_pairs={{0,448},{32,480},{64,0},{96,32},{128,64},{160,96},{192,128},{224,1... | collective-permute-start | bytes 884744 | tf_op jit(solution)/shard_map/ppermute | solution.py:411
  71.0 3.0 %collective-permute-start.11 = (bf16[128,1152]{1,0:T(8,128)(2,1)}, bf16[128,1152]{1,0:T(8,128)(2,1)}, u32[]{:S(2)}, u32[]{:S(2)}) collective-permute-start(bf16[128,1152]{1,0:T(8,128)(2,1)} %collective-permute-done.3.refs_4_), channel_id=1, source_target_pairs={{0,32},{32,0},{64,96},{96,64},{128,160},{160,128},{192,224},{224,1... | collective-permute-start | bytes 884744 | tf_op jit(solution)/shard_map/ppermute | solution.py:414
  75.6 5.2 %assemble.1 = (bf16[2048,1152]{1,0:T(8,128)(2,1)}, bf16[128,512]{1,0:T(8,128)(2,1)S(1)}, bf16[128,512]{1,0:T(8,128)(2,1)S(1)}) custom-call(s32[2]{0:T(128)S(1)} %pad_add_fusion.place_ref, f32[8,128]{1,0:T(8,128)S(1)} %copy-done.2, bf16[128,1152]{1,0:T(8,128)(2,1)} %get-tuple-element.41.refs_0_, bf16[128,1152]{1,0:T(8,128)(2,1)} %copy-done.3, ...), custom_call_target="tpu_custom_call" | custom-call | flops 327680 | bytes 4718592 | tf_op jit(solution)/shard_map/assemble/pallas_call | solution.py:41
  80.8 9.7 %all-to-all-done = bf16[32,8,6144]{2,1,0:T(8,128)(2,1)S(1)} async-done(((bf16[32,8,6144]{2,1,0:T(8,128)(2,1)}), bf16[32,8,6144]{2,1,0:T(8,128)(2,1)S(1)}, u32[]{:S(2)}, u32[]{:S(2)}) %all-to-all-start) | async-done | bytes 3145760 | tf_op jit(solution)/shard_map/all_to_all | solution.py:394
  90.4 7.3 %delta.1 = (bf16[384,768]{1,0:T(8,128)(2,1)S(1)}, bf16[384,128]{1,0:T(8,128)(2,1)S(1)}, bf16[768,384]{1,0:T(8,128)(2,1)S(1)}, bf16[384,2048]{1,0:T(8,128)(2,1)S(...) custom-call(s32[2]{0:T(128)S(1)} %pad_add_fusion.place_ref, bf16[256,6144]{1,0:T(8,128)(2,1)S(1)} %bitcast.18, ...), custom_call_target="tpu_custom_call" | custom-call | flops 2415919104 | bytes 6291456 | tf_op jit(solution)/shard_map/delta/pallas_call | solution.py:41
  97.7 6.0 %collective-permute-start.15 = (bf16[8,768,128]{2,1,0:T(8,128)(2,1)}, bf16[8,768,128]{2,1,0:T(8,128)(2,1)S(1)}, u32[]{:S(2)}, u32[]{:S(2)}) collective-permute-start(bf16[8,768,128]{2,1,0:T(8,128)(2,1)} %get-tuple-element.53), channel_id=1, source_target_pairs={{0,32},{32,0},{64,96},{96,64},{128,160},{160,128},{192,224},{224,1... | collective-permute-start | bytes 4718600 | tf_op jit(solution)/shard_map/ppermute | solution.py:414
  103.7 3.6 %slot_grad.1 = (bf16[256,3200]{1,0:T(8,128)(2,1)}, bf16[8,768,128]{2,1,0:T(8,128)(2,1)S(1)}) custom-call(s32[2]{0:T(128)S(1)} %pad_add_fusion.place_ref, bf16[384,768]{1,0:T(8,128)(2,1)S(1)} %get-tuple-element.46.delta_ref, bf16[384,128]{1,0:T(8,128)(2,1)S(1)} %get-tuple-element.47.prob_ref, bf16[768,384]{1,0:T(8,128)(2,1)S(1)} %get-tuple-element.48.delta_t_ref, ...), custom_call_target="tpu_custom_call" | custom-call | flops 1811939328 | bytes 6291456 | tf_op jit(solution)/shard_map/slot_grad/pallas_call | solution.py:41
  108.6 5.6 %all-to-all-start.1 = ((bf16[32,8,3200]{2,1,0:T(8,128)(2,1)}), bf16[32,8,3200]{2,1,0:T(8,128)(2,1)S(1)}, u32[]{:S(2)}, u32[]{:S(2)}) async-start(bf16[32,8,3200]{2,1,0:T(8,128)(2,1)} %bitcast.20), calls=%async_computation.1 | async-start | bytes 3276800 | tf_op jit(solution)/shard_map/all_to_all | solution.py:394
  114.3 7.5 %collective-permute-start.16 = (bf16[768,128]{1,0:T(8,128)(2,1)}, bf16[768,128]{1,0:T(8,128)(2,1)S(1)}, u32[]{:S(2)}, u32[]{:S(2)}) collective-permute-start(bf16[768,128]{1,0:T(8,128)(2,1)} %get-tuple-element.67), channel_id=1, source_target_pairs={{0,256},{32,288},{64,320},{96,352},{128,384},{160,416},{192,448},{... | collective-permute-start | bytes 589832 | tf_op jit(solution)/shard_map/ppermute | solution.py:411
  124.3 5.9 %collective-permute-start.18 = (bf16[768,128]{1,0:T(8,128)(2,1)}, bf16[768,128]{1,0:T(8,128)(2,1)S(1)}, u32[]{:S(2)}, u32[]{:S(2)}) collective-permute-start(bf16[768,128]{1,0:T(8,128)(2,1)} %get-tuple-element.69), channel_id=1, source_target_pairs={{0,320},{32,352},{64,384},{96,416},{128,448},{160,480},{192,0},{22... | collective-permute-start | bytes 589832 | tf_op jit(solution)/shard_map/ppermute | solution.py:411
  132.4 5.1 %collective-permute-start.20 = (bf16[768,128]{1,0:T(8,128)(2,1)}, bf16[768,128]{1,0:T(8,128)(2,1)S(1)}, u32[]{:S(2)}, u32[]{:S(2)}) collective-permute-start(bf16[768,128]{1,0:T(8,128)(2,1)} %get-tuple-element.71), channel_id=1, source_target_pairs={{0,384},{32,416},{64,448},{96,480},{128,0},{160,32},{192,64},{224,... | collective-permute-start | bytes 589832 | tf_op jit(solution)/shard_map/ppermute | solution.py:411
  139.7 4.0 %collective-permute-done.17.refs_2_ = bf16[768,128]{1,0:T(8,128)(2,1)S(1)} collective-permute-done((bf16[768,128]{1,0:T(8,128)(2,1)}, bf16[768,128]{1,0:T(8,128)(2,1)S(1)}, u32[]{:S(2)}, u32[]{:S(2)}) %collective-permute-start.17) | collective-permute-done | bytes 196640 | tf_op jit(solution)/shard_map/ppermute | solution.py:411
  145.7 3.5 %collective-permute-done.19.refs_4_ = bf16[768,128]{1,0:T(8,128)(2,1)S(1)} collective-permute-done((bf16[768,128]{1,0:T(8,128)(2,1)}, bf16[768,128]{1,0:T(8,128)(2,1)S(1)}, u32[]{:S(2)}, u32[]{:S(2)}) %collective-permute-start.19) | collective-permute-done | bytes 196640 | tf_op jit(solution)/shard_map/ppermute | solution.py:411
  149.2 3.8 %collective-permute-done.20.refs_5_ = bf16[768,128]{1,0:T(8,128)(2,1)S(1)} collective-permute-done((bf16[768,128]{1,0:T(8,128)(2,1)}, bf16[768,128]{1,0:T(8,128)(2,1)S(1)}, u32[]{:S(2)}, u32[]{:S(2)}) %collective-permute-start.20) | collective-permute-done | bytes 196640 | tf_op jit(solution)/shard_map/ppermute | solution.py:411
  153.0 3.8 %collective-permute-done.21.refs_6_ = bf16[768,128]{1,0:T(8,128)(2,1)S(1)} collective-permute-done((bf16[768,128]{1,0:T(8,128)(2,1)}, bf16[768,128]{1,0:T(8,128)(2,1)S(1)}, u32[]{:S(2)}, u32[]{:S(2)}) %collective-permute-start.21) | collective-permute-done | bytes 196640 | tf_op jit(solution)/shard_map/ppermute | solution.py:411
  (51 shorter events, 34.1 us)
Async XLA Ops:
  5.2 85.2 %all-to-all-start = ((bf16[32,8,6144]{2,1,0:T(8,128)(2,1)}), bf16[32,8,6144]{2,1,0:T(8,128)(2,1)S(1)}, u32[]{:S(2)}, u32[]{:S(2)}) async-start(bf16[32,8,6144]{2,1,0:T(8,128)(2,1)} %bitcast.19), calls=%async_computation | async-start | bytes 6291456 | tf_op jit(solution)/shard_map/all_to_all | solution.py:394
  21.9 11.7 %collective-permute-start = (bf16[128,1152]{1,0:T(8,128)(2,1)}, bf16[128,1152]{1,0:T(8,128)(2,1)S(1)}, u32[]{:S(2)}, u32[]{:S(2)}) collective-permute-start(bf16[128,1152]{1,0:T(8,128)(2,1)} %get-tuple-element.41.refs_0_), channel_id=1, source_target_pairs={{0,64},{32,96},{64,128},{96,160},{128,192},{160,224},{192,256},{22... | collective-permute-start | bytes 884744 | tf_op jit(solution)/shard_map/ppermute | solution.py:411
  25.1 10.4 %collective-permute-start.4 = (bf16[128,1152]{1,0:T(8,128)(2,1)}, bf16[128,1152]{1,0:T(8,128)(2,1)S(1)}, u32[]{:S(2)}, u32[]{:S(2)}) collective-permute-start(bf16[128,1152]{1,0:T(8,128)(2,1)} %get-tuple-element.41.refs_0_), channel_id=1, source_target_pairs={{0,448},{32,480},{64,0},{96,32},{128,64},{160,96},{192,128},{224,1... | collective-permute-start | bytes 884744 | tf_op jit(solution)/shard_map/ppermute | solution.py:411
  33.6 10.2 %collective-permute-start.1 = (bf16[128,1152]{1,0:T(8,128)(2,1)S(1)}, bf16[128,1152]{1,0:T(8,128)(2,1)}, u32[]{:S(2)}, u32[]{:S(2)}) collective-permute-start(bf16[128,1152]{1,0:T(8,128)(2,1)S(1)} %collective-permute-done.refs_1_), channel_id=1, source_target_pairs={{0,64},{32,96},{64,128},{96,160},{128,192},{160,224},{192,256},{22... | collective-permute-start | bytes 884744 | tf_op jit(solution)/shard_map/ppermute | solution.py:411
  35.6 18.9 %collective-permute-start.5 = (bf16[128,1152]{1,0:T(8,128)(2,1)S(1)}, bf16[128,1152]{1,0:T(8,128)(2,1)}, u32[]{:S(2)}, u32[]{:S(2)}) collective-permute-start(bf16[128,1152]{1,0:T(8,128)(2,1)S(1)} %collective-permute-done.4.refs_5_), channel_id=1, source_target_pairs={{0,448},{32,480},{64,0},{96,32},{128,64},{160,96},{192,128},{224,1... | collective-permute-start | bytes 884744 | tf_op jit(solution)/shard_map/ppermute | solution.py:411
  43.8 15.5 %collective-permute-start.2 = (bf16[128,1152]{1,0:T(8,128)(2,1)}, bf16[128,1152]{1,0:T(8,128)(2,1)}, u32[]{:S(2)}, u32[]{:S(2)}) collective-permute-start(bf16[128,1152]{1,0:T(8,128)(2,1)} %collective-permute-done.1.refs_2_), channel_id=1, source_target_pairs={{0,64},{32,96},{64,128},{96,160},{128,192},{160,224},{192,256},{22... | collective-permute-start | bytes 884744 | tf_op jit(solution)/shard_map/ppermute | solution.py:411
  45.7 15.6 %collective-permute-start.7 = (bf16[128,1152]{1,0:T(8,128)(2,1)}, bf16[128,1152]{1,0:T(8,128)(2,1)S(1)}, u32[]{:S(2)}, u32[]{:S(2)}) collective-permute-start(bf16[128,1152]{1,0:T(8,128)(2,1)} %get-tuple-element.41.refs_0_), channel_id=1, source_target_pairs={{0,32},{32,0},{64,96},{96,64},{128,160},{160,128},{192,224},{224,1... | collective-permute-start | bytes 884744 | tf_op jit(solution)/shard_map/ppermute | solution.py:414
  50.1 13.4 %collective-permute-start.12 = (bf16[128,1152]{1,0:T(8,128)(2,1)S(1)}, bf16[128,1152]{1,0:T(8,128)(2,1)S(1)}, u32[]{:S(2)}, u32[]{:S(2)}) collective-permute-start(bf16[128,1152]{1,0:T(8,128)(2,1)S(1)} %collective-permute-done.4.refs_5_), channel_id=1, source_target_pairs={{0,32},{32,0},{64,96},{96,64},{128,160},{160,128},{192,224},{224,1... | collective-permute-start | bytes 884744 | tf_op jit(solution)/shard_map/ppermute | solution.py:414
  52.0 13.6 %collective-permute-start.8 = (bf16[128,1152]{1,0:T(8,128)(2,1)S(1)}, bf16[128,1152]{1,0:T(8,128)(2,1)S(1)}, u32[]{:S(2)}, u32[]{:S(2)}) collective-permute-start(bf16[128,1152]{1,0:T(8,128)(2,1)S(1)} %collective-permute-done.refs_1_), channel_id=1, source_target_pairs={{0,32},{32,0},{64,96},{96,64},{128,160},{160,128},{192,224},{224,1... | collective-permute-start | bytes 884744 | tf_op jit(solution)/shard_map/ppermute | solution.py:414
  54.4 13.4 %collective-permute-start.6 = (bf16[128,1152]{1,0:T(8,128)(2,1)}, bf16[128,1152]{1,0:T(8,128)(2,1)}, u32[]{:S(2)}, u32[]{:S(2)}) collective-permute-start(bf16[128,1152]{1,0:T(8,128)(2,1)} %collective-permute-done.5.refs_6_), channel_id=1, source_target_pairs={{0,448},{32,480},{64,0},{96,32},{128,64},{160,96},{192,128},{224,1... | collective-permute-start | bytes 884744 | tf_op jit(solution)/shard_map/ppermute | solution.py:411
  59.3 11.7 %collective-permute-start.3 = (bf16[128,1152]{1,0:T(8,128)(2,1)}, bf16[128,1152]{1,0:T(8,128)(2,1)}, u32[]{:S(2)}, u32[]{:S(2)}) collective-permute-start(bf16[128,1152]{1,0:T(8,128)(2,1)} %collective-permute-done.2.refs_3_), channel_id=1, source_target_pairs={{0,64},{32,96},{64,128},{96,160},{128,192},{160,224},{192,256},{22... | collective-permute-start | bytes 884744 | tf_op jit(solution)/shard_map/ppermute | solution.py:411
  61.3 12.9 %collective-permute-start.13 = (bf16[128,1152]{1,0:T(8,128)(2,1)}, bf16[128,1152]{1,0:T(8,128)(2,1)}, u32[]{:S(2)}, u32[]{:S(2)}) collective-permute-start(bf16[128,1152]{1,0:T(8,128)(2,1)} %collective-permute-done.5.refs_6_), channel_id=1, source_target_pairs={{0,32},{32,0},{64,96},{96,64},{128,160},{160,128},{192,224},{224,1... | collective-permute-start | bytes 884744 | tf_op jit(solution)/shard_map/ppermute | solution.py:414
  63.5 10.7 %collective-permute-start.9 = (bf16[128,1152]{1,0:T(8,128)(2,1)}, bf16[128,1152]{1,0:T(8,128)(2,1)}, u32[]{:S(2)}, u32[]{:S(2)}) collective-permute-start(bf16[128,1152]{1,0:T(8,128)(2,1)} %collective-permute-done.1.refs_2_), channel_id=1, source_target_pairs={{0,32},{32,0},{64,96},{96,64},{128,160},{160,128},{192,224},{224,1... | collective-permute-start | bytes 884744 | tf_op jit(solution)/shard_map/ppermute | solution.py:414
  65.7 8.5 %collective-permute-start.10 = (bf16[128,1152]{1,0:T(8,128)(2,1)}, bf16[128,1152]{1,0:T(8,128)(2,1)}, u32[]{:S(2)}, u32[]{:S(2)}) collective-permute-start(bf16[128,1152]{1,0:T(8,128)(2,1)} %collective-permute-done.2.refs_3_), channel_id=1, source_target_pairs={{0,32},{32,0},{64,96},{96,64},{128,160},{160,128},{192,224},{224,1... | collective-permute-start | bytes 884744 | tf_op jit(solution)/shard_map/ppermute | solution.py:414
  67.9 6.3 %collective-permute-start.14 = (bf16[128,1152]{1,0:T(8,128)(2,1)}, bf16[128,1152]{1,0:T(8,128)(2,1)}, u32[]{:S(2)}, u32[]{:S(2)}) collective-permute-start(bf16[128,1152]{1,0:T(8,128)(2,1)} %collective-permute-done.6.refs_7_), channel_id=1, source_target_pairs={{0,32},{32,0},{64,96},{96,64},{128,160},{160,128},{192,224},{224,1... | collective-permute-start | bytes 884744 | tf_op jit(solution)/shard_map/ppermute | solution.py:414
  97.7 9.6 %collective-permute-start.15 = (bf16[8,768,128]{2,1,0:T(8,128)(2,1)}, bf16[8,768,128]{2,1,0:T(8,128)(2,1)S(1)}, u32[]{:S(2)}, u32[]{:S(2)}) collective-permute-start(bf16[8,768,128]{2,1,0:T(8,128)(2,1)} %get-tuple-element.53), channel_id=1, source_target_pairs={{0,32},{32,0},{64,96},{96,64},{128,160},{160,128},{192,224},{224,1... | collective-permute-start | bytes 4718600 | tf_op jit(solution)/shard_map/ppermute | solution.py:414
  108.6 49.6 %all-to-all-start.1 = ((bf16[32,8,3200]{2,1,0:T(8,128)(2,1)}), bf16[32,8,3200]{2,1,0:T(8,128)(2,1)S(1)}, u32[]{:S(2)}, u32[]{:S(2)}) async-start(bf16[32,8,3200]{2,1,0:T(8,128)(2,1)} %bitcast.20), calls=%async_computation.1 | async-start | bytes 3276800 | tf_op jit(solution)/shard_map/all_to_all | solution.py:394
  114.3 23.3 %collective-permute-start.16 = (bf16[768,128]{1,0:T(8,128)(2,1)}, bf16[768,128]{1,0:T(8,128)(2,1)S(1)}, u32[]{:S(2)}, u32[]{:S(2)}) collective-permute-start(bf16[768,128]{1,0:T(8,128)(2,1)} %get-tuple-element.67), channel_id=1, source_target_pairs={{0,256},{32,288},{64,320},{96,352},{128,384},{160,416},{192,448},{... | collective-permute-start | bytes 589832 | tf_op jit(solution)/shard_map/ppermute | solution.py:411
  121.8 22.0 %collective-permute-start.17 = (bf16[768,128]{1,0:T(8,128)(2,1)}, bf16[768,128]{1,0:T(8,128)(2,1)S(1)}, u32[]{:S(2)}, u32[]{:S(2)}) collective-permute-start(bf16[768,128]{1,0:T(8,128)(2,1)} %get-tuple-element.68), channel_id=1, source_target_pairs={{0,192},{32,224},{64,256},{96,288},{128,320},{160,352},{192,384},{... | collective-permute-start | bytes 589832 | tf_op jit(solution)/shard_map/ppermute | solution.py:411
  124.3 21.4 %collective-permute-start.18 = (bf16[768,128]{1,0:T(8,128)(2,1)}, bf16[768,128]{1,0:T(8,128)(2,1)S(1)}, u32[]{:S(2)}, u32[]{:S(2)}) collective-permute-start(bf16[768,128]{1,0:T(8,128)(2,1)} %get-tuple-element.69), channel_id=1, source_target_pairs={{0,320},{32,352},{64,384},{96,416},{128,448},{160,480},{192,0},{22... | collective-permute-start | bytes 589832 | tf_op jit(solution)/shard_map/ppermute | solution.py:411
  130.1 19.1 %collective-permute-start.19 = (bf16[768,128]{1,0:T(8,128)(2,1)}, bf16[768,128]{1,0:T(8,128)(2,1)S(1)}, u32[]{:S(2)}, u32[]{:S(2)}) collective-permute-start(bf16[768,128]{1,0:T(8,128)(2,1)} %get-tuple-element.70), channel_id=1, source_target_pairs={{0,128},{32,160},{64,192},{96,224},{128,256},{160,288},{192,320},{... | collective-permute-start | bytes 589832 | tf_op jit(solution)/shard_map/ppermute | solution.py:411
  132.4 20.6 %collective-permute-start.20 = (bf16[768,128]{1,0:T(8,128)(2,1)}, bf16[768,128]{1,0:T(8,128)(2,1)S(1)}, u32[]{:S(2)}, u32[]{:S(2)}) collective-permute-start(bf16[768,128]{1,0:T(8,128)(2,1)} %get-tuple-element.71), channel_id=1, source_target_pairs={{0,384},{32,416},{64,448},{96,480},{128,0},{160,32},{192,64},{224,... | collective-permute-start | bytes 589832 | tf_op jit(solution)/shard_map/ppermute | solution.py:411
  137.5 19.3 %collective-permute-start.21 = (bf16[768,128]{1,0:T(8,128)(2,1)}, bf16[768,128]{1,0:T(8,128)(2,1)S(1)}, u32[]{:S(2)}, u32[]{:S(2)}) collective-permute-start(bf16[768,128]{1,0:T(8,128)(2,1)} %get-tuple-element.72), channel_id=1, source_target_pairs={{0,64},{32,96},{64,128},{96,160},{128,192},{160,224},{192,256},{22... | collective-permute-start | bytes 589832 | tf_op jit(solution)/shard_map/ppermute | solution.py:411
  143.8 13.5 %collective-permute-start.22 = (bf16[768,128]{1,0:T(8,128)(2,1)}, bf16[768,128]{1,0:T(8,128)(2,1)S(1)}, u32[]{:S(2)}, u32[]{:S(2)}) collective-permute-start(bf16[768,128]{1,0:T(8,128)(2,1)} %get-tuple-element.73), channel_id=1, source_target_pairs={{0,448},{32,480},{64,0},{96,32},{128,64},{160,96},{192,128},{224,1... | collective-permute-start | bytes 589832 | tf_op jit(solution)/shard_map/ppermute | solution.py:411
  (9 other events, 236.2 us)

commit v2 on v1

--- a/solution.py
+++ b/solution.py
@@ -19,11 +19,15 @@
 near = pl.BlockSpec(memory_space=pltpu.VMEM)
 hbm = pl.BlockSpec(memory_space=pltpu.HBM)
 pins = {id(near): pltpu.VMEM, id(hbm): pltpu.HBM}
-smem = pl.BlockSpec(memory_space=pltpu.SMEM)
 
 
 def iota(shape, dim):
     return lax.broadcasted_iota(jnp.int32, shape, dim)
+
+
+def position():
+    me = lax.axis_index("dp")
+    return lax.shift_right_logical(me, 1), lax.bitwise_and(me, 1)
 
 
 def dot(a, b, dims=((1,), (0,))):
@@ -58,17 +62,19 @@
     return run
 
 
-def place_kernel(ids_ref, probs_ref, tokens_hbm, grads_hbm, out_hbm, target_ref, tokens, grads, out, sems):
+def place_kernel(
+    ids_hbm, probs_hbm, tokens_hbm, grads_hbm, out_hbm, target_hbm, ids_ref, probs_ref, tokens, grads, out, target, sems
+):
     count, width = tokens.shape
     half = width // 2
     slot_rows = out.shape[0]
     experts = slot_rows // main_slots
-    loads = [
-        pltpu.make_async_copy(tokens_hbm, tokens, sems.at[0]),
-        pltpu.make_async_copy(grads_hbm, grads, sems.at[1]),
-    ]
+    parts = ((ids_hbm, ids_ref), (probs_hbm, probs_ref), (tokens_hbm, tokens), (grads_hbm, grads))
+    loads = [pltpu.make_async_copy(x, y, sems.at[k]) for k, (x, y) in enumerate(parts)]
     for load in loads:
         load.start()
+    loads[0].wait()
+    loads[1].wait()
     ids = [ids_ref[k : k + 1, :] for k in range(2)]
     named = [(iota((experts, count), 0) == ids[k]).astype(f32) for k in range(2)]
     before = (iota((count, count), 0) < iota((count, count), 1)).astype(bf16)
@@ -83,16 +89,16 @@
         main_hit.append(row == main)
         tail_hit.append((row == tail, row == tail + tail_slots))
     probs = [probs_ref[k : k + 1, :].astype(f32) for k in range(2)]
-    target_ref[...] = jnp.concatenate([t.astype(f32) for t in targets] + probs + probs, axis=0)
+    target[...] = jnp.concatenate([t.astype(f32) for t in targets] + probs + probs, axis=0)
+    stores = [pltpu.make_async_copy(target, target_hbm, sems.at[4])]
+    stores[0].start()
 
     def placing(hit, scale):
         return (jnp.where(hit[0], scale[0], 0.0) + jnp.where(hit[1], scale[1], 0.0)).astype(bf16)
 
-    stores = []
-
     def store(start, size):
         span = (slice(None), pl.ds(start, size))
-        sem = sems.at[2 + len(stores)]
+        sem = sems.at[4 + len(stores)]
         stores.append(pltpu.make_async_copy(out.at[span], out_hbm.at[span], sem))
         stores[-1].start()
 
@@ -102,7 +108,7 @@
         tail = jnp.concatenate(
             [placing([tail_hit[k][side] for k in range(2)], scale) for side in range(2)], axis=1
         )
-        loads[at].wait()
+        loads[2 + at].wait()
         out[:, base : base + width] = dot(main, source[...]).astype(bf16)
         store(base, width)
         halves = jnp.concatenate([source[:, :half], source[:, half:]], axis=0)
@@ -154,12 +160,12 @@
     return (c == low).astype(bf16), (c == low + tail_slots).astype(bf16)
 
 
-def assemble_kernel(order, place_ref, target_ref, *refs):
+def assemble_kernel(order, target_ref, *refs):
     pieces = 2 * len(order)
     piece_refs = refs[:pieces]
-    weight_hbm, left_ref, right_ref, weight, sems = refs[pieces:]
+    weight_hbm, down_hbm, turned_hbm, left_ref, right_ref, weight, turned, sems = refs[pieces:]
     depth = piece_refs[0].shape[0]
-    y, core = place_ref[0], place_ref[1]
+    y, core = position()
     copies = []
     for k in range(pieces):
         origin = lax.rem(y + (len(order) - order[k % len(order)]), len(order))
@@ -180,14 +186,24 @@
     right_ref[:, slot_rows:] = high
     for copy in copies:
         copy.wait()
-    store = pltpu.make_async_copy(weight, weight_hbm, sems.at[pieces])
-    store.start()
-    store.wait()
-
-
-def weight_grads(place_ref, delta_t_ref, rows_ref, out, own, after):
+    gate_up = turned.shape[0]
+    stores = [
+        pltpu.make_async_copy(weight.at[:, pl.ds(0, gate_up)], weight_hbm, sems.at[0]),
+        pltpu.make_async_copy(weight.at[:, pl.ds(gate_up, gate_up // 2)], down_hbm, sems.at[1]),
+        pltpu.make_async_copy(turned, turned_hbm, sems.at[2]),
+    ]
+    stores[0].start()
+    stores[1].start()
+    for at in range(0, turned.shape[1], 2 * lane):
+        turned[:, at : at + 2 * lane] = weight[at : at + 2 * lane, :gate_up].T
+    stores[2].start()
+    for store in stores:
+        store.wait()
+
+
+def weight_grads(delta_t_ref, rows_ref, out, own, after):
     steps = out.shape[0]
-    y, core = place_ref[0], place_ref[1]
+    y, core = position()
     side = (core if own else 1 - core) * lane
 
     def columns(d):
@@ -202,15 +218,18 @@
 
 
 def delta_kernel(
-    place_ref,
     x_ref,
     weight_hbm,
+    down_hbm,
+    turned_hbm,
     delta_ref,
     prob_ref,
+    turned,
+    mine_ref,
+    other_hbm,
     delta_t_ref,
     rows,
     weight,
-    other_hbm,
     down,
     cotan,
     other,
@@ -222,14 +241,11 @@
     depth = width // weight_chunks
     spans = [slice(k * depth, (k + 1) * depth) for k in range(weight_chunks)]
     loads = [
-        pltpu.make_async_copy(weight_hbm.at[span, pl.ds(0, 2 * hidden)], weight.at[span], load_sems.at[k])
+        pltpu.make_async_copy(weight_hbm.at[span], weight.at[span], load_sems.at[k])
         for k, span in enumerate(spans)
     ]
-    loads.append(
-        pltpu.make_async_copy(
-            weight_hbm.at[:, pl.ds(2 * hidden, hidden)], down, load_sems.at[weight_chunks]
-        )
-    )
+    loads.append(pltpu.make_async_copy(down_hbm, down, load_sems.at[weight_chunks]))
+    loads.append(pltpu.make_async_copy(turned_hbm, turned, load_sems.at[weight_chunks + 1]))
     for load in loads:
         load.start()
     main_rows = x_ref.shape[0]
@@ -245,7 +261,7 @@
     for load, span in zip(loads, spans):
         load.wait()
         pre = pre + dot(rows[:, span], weight[span, :])
-    loads[-1].wait()
+    loads[-2].wait()
     grad = dot(cotan[...], down[...])
     gate_pre, up_pre = pre[:, :hidden], pre[:, hidden:]
     sig = jax.nn.sigmoid(gate_pre)
@@ -266,15 +282,14 @@
         stores.append(pltpu.make_async_copy(other.at[span], other_hbm.at[span], sems.at[d // 2]))
         stores[-1].start()
 
-    weight_grads(place_ref, delta_t_ref, rows, other, False, after)
-    for copy in stores:
+    weight_grads(delta_t_ref, rows, other, False, after)
+    weight_grads(delta_t_ref, rows, mine_ref, True, lambda d: None)
+    for copy in stores + loads[-1:]:
         copy.wait()
 
 
-def slot_grad_kernel(
-    place_ref, delta_ref, prob_ref, delta_t_ref, rows_ref, weight_ref, out_hbm, mine_ref, out, sems
-):
-    width = weight_ref.shape[0]
+def slot_grad_kernel(delta_ref, prob_ref, turned_ref, out_hbm, out, sems):
+    width = turned_ref.shape[1]
     half = width // 2
     main_rows = out.shape[0]
     tail_rows = delta_ref.shape[0] - main_rows
@@ -290,7 +305,7 @@
     tails = []
     for at in range(2):
         span = slice(at * half, (at + 1) * half)
-        back = dot(delta_ref[...], weight_ref[span, :], ((1,), (1,))).astype(bf16)
+        back = dot(delta_ref[...], turned_ref[:, span]).astype(bf16)
         out[:, span] = back[:main_rows]
         store(at * half, half)
         tails.append(back[main_rows:])
@@ -301,7 +316,6 @@
     probs = jnp.where(at_lane == 1, late, prob_ref[:main_rows, :].astype(f32))
     out[:, width + half :] = probs.astype(bf16)
     store(width, half + lane)
-    weight_grads(place_ref, delta_t_ref, rows_ref, mine_ref, True, lambda d: None)
     for copy in stores:
         copy.wait()
 
@@ -368,22 +382,23 @@
     ny = dp // 2
     slot_rows = experts * main_slots
     all_rows = experts * (main_slots + tail_slots)
-    me = lax.axis_index("dp")
-    here = jnp.stack([lax.shift_right_logical(me, 1), lax.bitwise_and(me, 1)])
     sds = jax.ShapeDtypeStruct
     ids, probs = expert_ids.T, route_probs.T
 
     sent, targets = call(
         place_kernel,
         (sds((slot_rows, 3 * width), bf16), sds((8, count), f32)),
-        [vmem, vmem, hbm, hbm],
-        (hbm, vmem),
+        [hbm] * 4,
+        (hbm, hbm),
         (slot_rows * count * width * 10, 5 * slot_rows * width * 2),
         scratch=(
+            pltpu.VMEM((2, count), jnp.int32),
+            pltpu.VMEM((2, count), bf16),
             pltpu.VMEM((count, width), bf16),
             pltpu.VMEM((count, width), bf16),
             pltpu.VMEM((slot_rows, 3 * width), bf16),
-            pltpu.SemaphoreType.DMA((6,)),
+            pltpu.VMEM((8, count), f32),
+            pltpu.SemaphoreType.DMA((9,)),
         ),
         name="place",
         mib=large,
@@ -420,57 +435,66 @@
     held = [(0, piece)] + [(d, forward[d]) for d in range(1, ny // 2 + 1)]
     held += [(ny - d, backward[d]) for d in range(1, ny // 2)]
     other = [across(x) for _, x in held]
-    weights, place_left, place_right = call(
+    gate_up, down, turned, place_left, place_right = call(
         functools.partial(assemble_kernel, [d for d, _ in held]),
-        (sds((width, 3 * hidden), bf16),) + (sds((count, 2 * slot_rows), bf16),) * 2,
-        [smem, vmem] + [hbm] * dp,
-        (hbm, vmem, vmem),
+        (
+            sds((width, 2 * hidden), bf16),
+            sds((width, hidden), bf16),
+            sds((2 * hidden, width), bf16),
+        )
+        + (sds((count, 2 * slot_rows), bf16),) * 2,
+        [vmem] + [hbm] * dp,
+        (hbm, hbm, hbm, vmem, vmem),
         (count * slot_rows * 10, 6 * width * hidden),
         scratch=(
             pltpu.VMEM((width, 3 * hidden), bf16),
-            pltpu.SemaphoreType.DMA((dp + 1,)),
+            pltpu.VMEM((2 * hidden, width), bf16),
+            pltpu.SemaphoreType.DMA((dp,)),
         ),
         name="assemble",
-    )(here, targets, *[x for _, x in held], *other)
+        mib=24,
+    )(targets, *[x for _, x in held], *other)
 
     block = (2 * hidden, lane)
-    delta, slot_probs, delta_t, rows, gate_up, theirs = call(
+    delta, slot_probs, turned, mine, theirs = call(
         delta_kernel,
         (
             sds((all_rows, 2 * hidden), bf16),
             sds((all_rows, lane), bf16),
-            sds((2 * hidden, all_rows), bf16),
-            sds((all_rows, width), bf16),
-            sds((width, 2 * hidden), bf16),
+            sds((2 * hidden, width), bf16),
+            sds((ny, *block), bf16),
             sds((ny, *block), bf16),
         ),
-        [smem, vmem, hbm],
-        (near,) * 5 + (hbm,),
-        (all_rows * width * hidden * 8, 12 * slot_rows * width),
+        [vmem, hbm, hbm, hbm],
+        (near,) * 4 + (hbm,),
+        (all_rows * width * hidden * 10, 12 * slot_rows * width),
         scratch=(
+            pltpu.VMEM((2 * hidden, all_rows), bf16),
+            pltpu.VMEM((all_rows, width), bf16),
+            pltpu.VMEM((width, 2 * hidden), bf16),
             pltpu.VMEM((width, hidden), bf16),
             pltpu.VMEM((all_rows, width), bf16),
             pltpu.VMEM((ny, *block), bf16),
             pltpu.SemaphoreType.DMA((ny // 2,)),
-            pltpu.SemaphoreType.DMA((weight_chunks + 1,)),
+            pltpu.SemaphoreType.DMA((weight_chunks + 2,)),
         ),
         name="delta",
         mib=24,
-    )(here, arrived, weights)
+    )(arrived, gate_up, down, turned)
     got = across(theirs)
-    returned, mine = call(
+    returned = call(
         slot_grad_kernel,
-        (sds((slot_rows, width + half + lane), bf16), sds((ny, *block), bf16)),
-        [smem] + [near] * 5,
-        (hbm, near),
-        (all_rows * width * hidden * 6, 12 * slot_rows * width),
+        (sds((slot_rows, width + half + lane), bf16),),
+        [near] * 3,
+        (hbm,),
+        (all_rows * width * hidden * 4, 12 * slot_rows * width),
         scratch=(
             pltpu.VMEM((slot_rows, width + half + lane), bf16),
             pltpu.SemaphoreType.DMA((3,)),
         ),
         name="slot_grad",
         mib=24,
-    )(here, delta, slot_probs, delta_t, rows, gate_up)
+    )(delta, slot_probs, turned)[0]
     sums = call(
         pair_sum_kernel,
         (sds(block, bf16),) * ny,

time: 160 us -> 159 us (level)
  Pallas kernels: 27 us -> 25.1 us
    pallas_call x8, Pallas kernels: 27 us -> 25.1 us  [run(): return kernel_call(*pinned)]
  transfers between devices with their start and end apart: 25 -> 25, of which waited for: 10 -> 11; matrix products, arithmetic and copies ran while one was open for 0% -> 0% of each run, Pallas kernels for 8% -> 8%
where the time goes in v2:
time: 159 us; the launch traced here: 158 us
  starting transfers between devices  95.3 us (60%)
  waiting for transfers between devices  35.6 us (22%)
  Pallas kernels  25.1 us (16%)
    ppermute x14, starting transfers between devices, along_y(): return lax.ppermute(x, 'dp', moves)  49.6 us
    ppermute x9, starting transfers between devices, across(): return lax.ppermute(x, 'dp', [(i, i ^ 1) for i in range(dp)])  26.4 us
    pallas_call x8, Pallas kernels, run(): return kernel_call(*pinned)  25.1 us
    ppermute x14, waiting for transfers between devices, along_y(): return lax.ppermute(x, 'dp', moves)  24.6 us
    all_to_all x2, starting transfers between devices, exchange(): lax.all_to_all(blocks, 'expert', split_axis=0, concat_axis=0, tiled=True)  19.4 us
    all_to_all x2, waiting for transfers between devices, exchange(): lax.all_to_all(blocks, 'expert', split_axis=0, concat_axis=0, tiled=True)  9.28 us
  transfers between devices with their start and end apart: 25, of which 11 were waited for; matrix products, arithmetic and copies ran while one was open for 0% of the time, Pallas kernels for 8%

profile of v2, /device:TPU:1, one launch (start us, length us, event | category | flops | bytes accessed | tf_op | source)
XLA Modules:
  0.0 158.0 jit_solution(17929936469512489254)
XLA Ops:
  0.6 3.3 %place.1 = (bf16[256,6144]{1,0:T(8,128)(2,1)}, f32[8,128]{1,0:T(8,128)}) custom-call(s32[2,128]{1,0:T(2,128)} %bitcast.27, bf16[2,128]{1,0:T(2,128)(2,1)} %bitcast.28, bf16[128,2048]{1,0:T(8,128)(2,1)} %tokens_hbm.1, bf16[128,2048]{1,0:T(8,128)(2,1)} %grads_hbm.1), custom_call_target="tpu_custom_call" | custom-call | flops 671088640 | bytes 5242880 | tf_op jit(solution)/shard_map/place/pallas_call | solution.py:45
  4.0 13.7 %all-to-all-start = ((bf16[32,8,6144]{2,1,0:T(8,128)(2,1)}), bf16[32,8,6144]{2,1,0:T(8,128)(2,1)S(1)}, u32[]{:S(2)}, u32[]{:S(2)}) async-start(bf16[32,8,6144]{2,1,0:T(8,128)(2,1)} %bitcast.18), calls=%async_computation | async-start | bytes 6291456 | tf_op jit(solution)/shard_map/all_to_all | solution.py:409
  17.7 2.9 %mask.1 = (bf16[128,1152]{1,0:T(8,128)(2,1)}, f32[128,768]{1,0:T(8,128)}) custom-call(bf16[128,384]{1,0:T(8,128)(2,1)} %bitcast.19, bf16[128,384]{1,0:T(8,128)(2,1)} %bitcast.20, bf16[384,128]{1,0:T(8,128)(2,1)} %bitcast.21, s32[32,384]{1,0:T(8,128)} %bitcast.22, s32[32,384]{1,0:T(8,128)} %bitcast.23, s32[96,128]{1,0:T(8,128)} %bitcast.24), custom_call_target="tpu_custom_call" | custom-call | flops 78643200 | bytes 294912 | tf_op jit(solution)/shard_map/mask/pallas_call | solution.py:45
  20.7 3.2 %collective-permute-start = (bf16[128,1152]{1,0:T(8,128)(2,1)}, bf16[128,1152]{1,0:T(8,128)(2,1)S(1)}, u32[]{:S(2)}, u32[]{:S(2)}) collective-permute-start(bf16[128,1152]{1,0:T(8,128)(2,1)} %get-tuple-element.40.refs_0_), channel_id=1, source_target_pairs={{0,64},{32,96},{64,128},{96,160},{128,192},{160,224},{192,256},{22... | collective-permute-start | bytes 884744 | tf_op jit(solution)/shard_map/ppermute | solution.py:426
  23.9 3.8 %collective-permute-start.4 = (bf16[128,1152]{1,0:T(8,128)(2,1)}, bf16[128,1152]{1,0:T(8,128)(2,1)S(1)}, u32[]{:S(2)}, u32[]{:S(2)}) collective-permute-start(bf16[128,1152]{1,0:T(8,128)(2,1)} %get-tuple-element.40.refs_0_), channel_id=1, source_target_pairs={{0,448},{32,480},{64,0},{96,32},{128,64},{160,96},{192,128},{224,1... | collective-permute-start | bytes 884744 | tf_op jit(solution)/shard_map/ppermute | solution.py:426
  27.7 4.7 %collective-permute-done.refs_1_ = bf16[128,1152]{1,0:T(8,128)(2,1)S(1)} collective-permute-done((bf16[128,1152]{1,0:T(8,128)(2,1)}, bf16[128,1152]{1,0:T(8,128)(2,1)S(1)}, u32[]{:S(2)}, u32[]{:S(2)}) %collective-permute-start) | collective-permute-done | bytes 294944 | tf_op jit(solution)/shard_map/ppermute | solution.py:426
  34.3 4.6 %collective-permute-start.5 = (bf16[128,1152]{1,0:T(8,128)(2,1)S(1)}, bf16[128,1152]{1,0:T(8,128)(2,1)S(1)}, u32[]{:S(2)}, u32[]{:S(2)}) collective-permute-start(bf16[128,1152]{1,0:T(8,128)(2,1)S(1)} %collective-permute-done.4.refs_5_), channel_id=1, source_target_pairs={{0,448},{32,480},{64,0},{96,32},{128,64},{160,96},{192,128},{224,1... | collective-permute-start | bytes 884744 | tf_op jit(solution)/shard_map/ppermute | solution.py:426
  38.9 3.5 %collective-permute-done.1.refs_2_ = bf16[128,1152]{1,0:T(8,128)(2,1)S(1)} collective-permute-done((bf16[128,1152]{1,0:T(8,128)(2,1)S(1)}, bf16[128,1152]{1,0:T(8,128)(2,1)S(1)}, u32[]{:S(2)}, u32[]{:S(2)}) %collective-permute-start.1) | collective-permute-done | bytes 294944 | tf_op jit(solution)/shard_map/ppermute | solution.py:426
  44.4 4.4 %collective-permute-start.7 = (bf16[128,1152]{1,0:T(8,128)(2,1)}, bf16[128,1152]{1,0:T(8,128)(2,1)S(1)}, u32[]{:S(2)}, u32[]{:S(2)}) collective-permute-start(bf16[128,1152]{1,0:T(8,128)(2,1)} %get-tuple-element.40.refs_0_), channel_id=1, source_target_pairs={{0,32},{32,0},{64,96},{96,64},{128,160},{160,128},{192,224},{224,1... | collective-permute-start | bytes 884744 | tf_op jit(solution)/shard_map/ppermute | solution.py:429
  53.1 4.9 %collective-permute-start.6 = (bf16[128,1152]{1,0:T(8,128)(2,1)S(1)}, bf16[128,1152]{1,0:T(8,128)(2,1)S(1)}, u32[]{:S(2)}, u32[]{:S(2)}) collective-permute-start(bf16[128,1152]{1,0:T(8,128)(2,1)S(1)} %collective-permute-done.5.refs_6_), channel_id=1, source_target_pairs={{0,448},{32,480},{64,0},{96,32},{128,64},{160,96},{192,128},{224,1... | collective-permute-start | bytes 884744 | tf_op jit(solution)/shard_map/ppermute | solution.py:426
  69.4 3.0 %collective-permute-start.11 = (bf16[128,1152]{1,0:T(8,128)(2,1)S(1)}, bf16[128,1152]{1,0:T(8,128)(2,1)S(1)}, u32[]{:S(2)}, u32[]{:S(2)}) collective-permute-start(bf16[128,1152]{1,0:T(8,128)(2,1)S(1)} %collective-permute-done.3.refs_4_), channel_id=1, source_target_pairs={{0,32},{32,0},{64,96},{96,64},{128,160},{160,128},{192,224},{224,1... | collective-permute-start | bytes 884744 | tf_op jit(solution)/shard_map/ppermute | solution.py:429
  74.3 5.6 %assemble.1 = (bf16[2048,768]{1,0:T(8,128)(2,1)}, bf16[2048,384]{1,0:T(8,128)(2,1)}, bf16[768,2048]{1,0:T(8,128)(2,1)}, bf16[128,512]{1,0:T(8,128)(2,1)S(1)}, bf16[128,512]{1,0:T(8,128)(2,1)S(1)}) custom-call(f32[8,128]{1,0:T(8,128)S(1)} %copy-done.2, bf16[128,1152]{1,0:T(8,128)(2,1)} %get-tuple-element.40.refs_0_, bf16[128,1152]{1,0:T(8,128)(2,1)} %copy-done.3, ...), custom_call_target="tpu_custom_call" | custom-call | flops 327680 | bytes 4718592 | tf_op jit(solution)/shard_map/assemble/pallas_call | solution.py:45
  80.0 9.3 %all-to-all-done = bf16[32,8,6144]{2,1,0:T(8,128)(2,1)S(1)} async-done(((bf16[32,8,6144]{2,1,0:T(8,128)(2,1)}), bf16[32,8,6144]{2,1,0:T(8,128)(2,1)S(1)}, u32[]{:S(2)}, u32[]{:S(2)}) %all-to-all-start) | async-done | bytes 3145760 | tf_op jit(solution)/shard_map/all_to_all | solution.py:409
  89.2 7.1 %delta.1 = (bf16[384,768]{1,0:T(8,128)(2,1)S(1)}, bf16[384,128]{1,0:T(8,128)(2,1)S(1)}, bf16[768,2048]{1,0:T(8,128)(2,1)S(1)}, bf16[8,768,128]{2,1,0:T(8,128)(2,1)S(1)}, bf16[8,768,128]{2,1,0:T(8,128)(2,1)}) custom-call(bf16[256,6144]{1,0:T(8,128)(2,1)S(1)} %bitcast.16, bf16[2048,768]{1,0:T(8,128)(2,1)} %get-tuple-element.44.weight_hbm, ...), custom_call_target="tpu_custom_call" | custom-call | flops 3019898880 | bytes 6291456 | tf_op jit(solution)/shard_map/delta/pallas_call | solution.py:45
  96.4 6.0 %collective-permute-start.15 = (bf16[8,768,128]{2,1,0:T(8,128)(2,1)}, bf16[8,768,128]{2,1,0:T(8,128)(2,1)S(1)}, u32[]{:S(2)}, u32[]{:S(2)}) collective-permute-start(bf16[8,768,128]{2,1,0:T(8,128)(2,1)} %get-tuple-element.51), channel_id=1, source_target_pairs={{0,32},{32,0},{64,96},{96,64},{128,160},{160,128},{192,224},{224,1... | collective-permute-start | bytes 4718600 | tf_op jit(solution)/shard_map/ppermute | solution.py:429
  102.4 2.6 %slot_grad.1 = bf16[256,3200]{1,0:T(8,128)(2,1)} custom-call(bf16[384,768]{1,0:T(8,128)(2,1)S(1)} %get-tuple-element.47.delta_ref, bf16[384,128]{1,0:T(8,128)(2,1)S(1)} %get-tuple-element.48.prob_ref, bf16[768,2048]{1,0:T(8,128)(2,1)S(1)} %get-tuple-element.49.turned_ref), custom_call_target="tpu_custom_call" | custom-call | flops 1207959552 | bytes 6291456 | tf_op jit(solution)/shard_map/slot_grad/pallas_call | solution.py:45
  106.9 5.7 %all-to-all-start.1 = ((bf16[32,8,3200]{2,1,0:T(8,128)(2,1)}), bf16[32,8,3200]{2,1,0:T(8,128)(2,1)S(1)}, u32[]{:S(2)}, u32[]{:S(2)}) async-start(bf16[32,8,3200]{2,1,0:T(8,128)(2,1)} %bitcast.17), calls=%async_computation.1 | async-start | bytes 3276800 | tf_op jit(solution)/shard_map/all_to_all | solution.py:409
  112.6 7.4 %collective-permute-start.16 = (bf16[768,128]{1,0:T(8,128)(2,1)}, bf16[768,128]{1,0:T(8,128)(2,1)S(1)}, u32[]{:S(2)}, u32[]{:S(2)}) collective-permute-start(bf16[768,128]{1,0:T(8,128)(2,1)} %get-tuple-element.65), channel_id=1, source_target_pairs={{0,256},{32,288},{64,320},{96,352},{128,384},{160,416},{192,448},{... | collective-permute-start | bytes 589832 | tf_op jit(solution)/shard_map/ppermute | solution.py:426
  122.6 5.7 %collective-permute-start.18 = (bf16[768,128]{1,0:T(8,128)(2,1)S(1)}, bf16[768,128]{1,0:T(8,128)(2,1)S(1)}, u32[]{:S(2)}, u32[]{:S(2)}) collective-permute-start(bf16[768,128]{1,0:T(8,128)(2,1)S(1)} %copy-done.22), channel_id=1, source_target_pairs={{0,320},{32,352},{64,384},{96,416},{128,448},{160,480},{192,0},{22... | collective-permute-start | bytes 589832 | tf_op jit(solution)/shard_map/ppermute | solution.py:426
  130.9 4.8 %collective-permute-start.20 = (bf16[768,128]{1,0:T(8,128)(2,1)S(1)}, bf16[768,128]{1,0:T(8,128)(2,1)S(1)}, u32[]{:S(2)}, u32[]{:S(2)}) collective-permute-start(bf16[768,128]{1,0:T(8,128)(2,1)S(1)} %copy-done.20), channel_id=1, source_target_pairs={{0,384},{32,416},{64,448},{96,480},{128,0},{160,32},{192,64},{224,... | collective-permute-start | bytes 589832 | tf_op jit(solution)/shard_map/ppermute | solution.py:426
  138.2 4.6 %collective-permute-done.17.refs_2_ = bf16[768,128]{1,0:T(8,128)(2,1)S(1)} collective-permute-done((bf16[768,128]{1,0:T(8,128)(2,1)}, bf16[768,128]{1,0:T(8,128)(2,1)S(1)}, u32[]{:S(2)}, u32[]{:S(2)}) %collective-permute-start.17) | collective-permute-done | bytes 196640 | tf_op jit(solution)/shard_map/ppermute | solution.py:426
  144.8 2.9 %collective-permute-done.19.refs_4_ = bf16[768,128]{1,0:T(8,128)(2,1)S(1)} collective-permute-done((bf16[768,128]{1,0:T(8,128)(2,1)S(1)}, bf16[768,128]{1,0:T(8,128)(2,1)S(1)}, u32[]{:S(2)}, u32[]{:S(2)}) %collective-permute-start.19) | collective-permute-done | bytes 196640 | tf_op jit(solution)/shard_map/ppermute | solution.py:426
  147.6 3.9 %collective-permute-done.20.refs_5_ = bf16[768,128]{1,0:T(8,128)(2,1)S(1)} collective-permute-done((bf16[768,128]{1,0:T(8,128)(2,1)S(1)}, bf16[768,128]{1,0:T(8,128)(2,1)S(1)}, u32[]{:S(2)}, u32[]{:S(2)}) %collective-permute-start.20) | collective-permute-done | bytes 196640 | tf_op jit(solution)/shard_map/ppermute | solution.py:426
  151.5 3.1 %collective-permute-done.21.refs_6_ = bf16[768,128]{1,0:T(8,128)(2,1)S(1)} collective-permute-done((bf16[768,128]{1,0:T(8,128)(2,1)S(1)}, bf16[768,128]{1,0:T(8,128)(2,1)S(1)}, u32[]{:S(2)}, u32[]{:S(2)}) %collective-permute-start.21) | collective-permute-done | bytes 196640 | tf_op jit(solution)/shard_map/ppermute | solution.py:426
  (80 shorter events, 35.9 us)
Async XLA Ops:
  4.0 85.2 %all-to-all-start = ((bf16[32,8,6144]{2,1,0:T(8,128)(2,1)}), bf16[32,8,6144]{2,1,0:T(8,128)(2,1)S(1)}, u32[]{:S(2)}, u32[]{:S(2)}) async-start(bf16[32,8,6144]{2,1,0:T(8,128)(2,1)} %bitcast.18), calls=%async_computation | async-start | bytes 6291456 | tf_op jit(solution)/shard_map/all_to_all | solution.py:409
  20.7 11.7 %collective-permute-start = (bf16[128,1152]{1,0:T(8,128)(2,1)}, bf16[128,1152]{1,0:T(8,128)(2,1)S(1)}, u32[]{:S(2)}, u32[]{:S(2)}) collective-permute-start(bf16[128,1152]{1,0:T(8,128)(2,1)} %get-tuple-element.40.refs_0_), channel_id=1, source_target_pairs={{0,64},{32,96},{64,128},{96,160},{128,192},{160,224},{192,256},{22... | collective-permute-start | bytes 884744 | tf_op jit(solution)/shard_map/ppermute | solution.py:426
  23.9 10.4 %collective-permute-start.4 = (bf16[128,1152]{1,0:T(8,128)(2,1)}, bf16[128,1152]{1,0:T(8,128)(2,1)S(1)}, u32[]{:S(2)}, u32[]{:S(2)}) collective-permute-start(bf16[128,1152]{1,0:T(8,128)(2,1)} %get-tuple-element.40.refs_0_), channel_id=1, source_target_pairs={{0,448},{32,480},{64,0},{96,32},{128,64},{160,96},{192,128},{224,1... | collective-permute-start | bytes 884744 | tf_op jit(solution)/shard_map/ppermute | solution.py:426
  32.4 10.0 %collective-permute-start.1 = (bf16[128,1152]{1,0:T(8,128)(2,1)S(1)}, bf16[128,1152]{1,0:T(8,128)(2,1)S(1)}, u32[]{:S(2)}, u32[]{:S(2)}) collective-permute-start(bf16[128,1152]{1,0:T(8,128)(2,1)S(1)} %collective-permute-done.refs_1_), channel_id=1, source_target_pairs={{0,64},{32,96},{64,128},{96,160},{128,192},{160,224},{192,256},{22... | collective-permute-start | bytes 884744 | tf_op jit(solution)/shard_map/ppermute | solution.py:426
  34.3 18.8 %collective-permute-start.5 = (bf16[128,1152]{1,0:T(8,128)(2,1)S(1)}, bf16[128,1152]{1,0:T(8,128)(2,1)S(1)}, u32[]{:S(2)}, u32[]{:S(2)}) collective-permute-start(bf16[128,1152]{1,0:T(8,128)(2,1)S(1)} %collective-permute-done.4.refs_5_), channel_id=1, source_target_pairs={{0,448},{32,480},{64,0},{96,32},{128,64},{160,96},{192,128},{224,1... | collective-permute-start | bytes 884744 | tf_op jit(solution)/shard_map/ppermute | solution.py:426
  42.4 15.5 %collective-permute-start.2 = (bf16[128,1152]{1,0:T(8,128)(2,1)S(1)}, bf16[128,1152]{1,0:T(8,128)(2,1)S(1)}, u32[]{:S(2)}, u32[]{:S(2)}) collective-permute-start(bf16[128,1152]{1,0:T(8,128)(2,1)S(1)} %collective-permute-done.1.refs_2_), channel_id=1, source_target_pairs={{0,64},{32,96},{64,128},{96,160},{128,192},{160,224},{192,256},{22... | collective-permute-start | bytes 884744 | tf_op jit(solution)/shard_map/ppermute | solution.py:426
  44.4 15.6 %collective-permute-start.7 = (bf16[128,1152]{1,0:T(8,128)(2,1)}, bf16[128,1152]{1,0:T(8,128)(2,1)S(1)}, u32[]{:S(2)}, u32[]{:S(2)}) collective-permute-start(bf16[128,1152]{1,0:T(8,128)(2,1)} %get-tuple-element.40.refs_0_), channel_id=1, source_target_pairs={{0,32},{32,0},{64,96},{96,64},{128,160},{160,128},{192,224},{224,1... | collective-permute-start | bytes 884744 | tf_op jit(solution)/shard_map/ppermute | solution.py:429
  48.7 13.4 %collective-permute-start.12 = (bf16[128,1152]{1,0:T(8,128)(2,1)S(1)}, bf16[128,1152]{1,0:T(8,128)(2,1)S(1)}, u32[]{:S(2)}, u32[]{:S(2)}) collective-permute-start(bf16[128,1152]{1,0:T(8,128)(2,1)S(1)} %collective-permute-done.4.refs_5_), channel_id=1, source_target_pairs={{0,32},{32,0},{64,96},{96,64},{128,160},{160,128},{192,224},{224,1... | collective-permute-start | bytes 884744 | tf_op jit(solution)/shard_map/ppermute | solution.py:429
  50.7 13.6 %collective-permute-start.8 = (bf16[128,1152]{1,0:T(8,128)(2,1)S(1)}, bf16[128,1152]{1,0:T(8,128)(2,1)S(1)}, u32[]{:S(2)}, u32[]{:S(2)}) collective-permute-start(bf16[128,1152]{1,0:T(8,128)(2,1)S(1)} %collective-permute-done.refs_1_), channel_id=1, source_target_pairs={{0,32},{32,0},{64,96},{96,64},{128,160},{160,128},{192,224},{224,1... | collective-permute-start | bytes 884744 | tf_op jit(solution)/shard_map/ppermute | solution.py:429
  53.1 13.4 %collective-permute-start.6 = (bf16[128,1152]{1,0:T(8,128)(2,1)S(1)}, bf16[128,1152]{1,0:T(8,128)(2,1)S(1)}, u32[]{:S(2)}, u32[]{:S(2)}) collective-permute-start(bf16[128,1152]{1,0:T(8,128)(2,1)S(1)} %collective-permute-done.5.refs_6_), channel_id=1, source_target_pairs={{0,448},{32,480},{64,0},{96,32},{128,64},{160,96},{192,128},{224,1... | collective-permute-start | bytes 884744 | tf_op jit(solution)/shard_map/ppermute | solution.py:426
  58.0 11.4 %collective-permute-start.3 = (bf16[128,1152]{1,0:T(8,128)(2,1)S(1)}, bf16[128,1152]{1,0:T(8,128)(2,1)S(1)}, u32[]{:S(2)}, u32[]{:S(2)}) collective-permute-start(bf16[128,1152]{1,0:T(8,128)(2,1)S(1)} %collective-permute-done.2.refs_3_), channel_id=1, source_target_pairs={{0,64},{32,96},{64,128},{96,160},{128,192},{160,224},{192,256},{22... | collective-permute-start | bytes 884744 | tf_op jit(solution)/shard_map/ppermute | solution.py:426
  59.9 12.5 %collective-permute-start.13 = (bf16[128,1152]{1,0:T(8,128)(2,1)S(1)}, bf16[128,1152]{1,0:T(8,128)(2,1)S(1)}, u32[]{:S(2)}, u32[]{:S(2)}) collective-permute-start(bf16[128,1152]{1,0:T(8,128)(2,1)S(1)} %collective-permute-done.5.refs_6_), channel_id=1, source_target_pairs={{0,32},{32,0},{64,96},{96,64},{128,160},{160,128},{192,224},{224,1... | collective-permute-start | bytes 884744 | tf_op jit(solution)/shard_map/ppermute | solution.py:429
  62.2 10.3 %collective-permute-start.9 = (bf16[128,1152]{1,0:T(8,128)(2,1)S(1)}, bf16[128,1152]{1,0:T(8,128)(2,1)S(1)}, u32[]{:S(2)}, u32[]{:S(2)}) collective-permute-start(bf16[128,1152]{1,0:T(8,128)(2,1)S(1)} %collective-permute-done.1.refs_2_), channel_id=1, source_target_pairs={{0,32},{32,0},{64,96},{96,64},{128,160},{160,128},{192,224},{224,1... | collective-permute-start | bytes 884744 | tf_op jit(solution)/shard_map/ppermute | solution.py:429
  64.3 8.2 %collective-permute-start.10 = (bf16[128,1152]{1,0:T(8,128)(2,1)S(1)}, bf16[128,1152]{1,0:T(8,128)(2,1)S(1)}, u32[]{:S(2)}, u32[]{:S(2)}) collective-permute-start(bf16[128,1152]{1,0:T(8,128)(2,1)S(1)} %collective-permute-done.2.refs_3_), channel_id=1, source_target_pairs={{0,32},{32,0},{64,96},{96,64},{128,160},{160,128},{192,224},{224,1... | collective-permute-start | bytes 884744 | tf_op jit(solution)/shard_map/ppermute | solution.py:429
  66.5 5.9 %collective-permute-start.14 = (bf16[128,1152]{1,0:T(8,128)(2,1)S(1)}, bf16[128,1152]{1,0:T(8,128)(2,1)S(1)}, u32[]{:S(2)}, u32[]{:S(2)}) collective-permute-start(bf16[128,1152]{1,0:T(8,128)(2,1)S(1)} %collective-permute-done.6.refs_7_), channel_id=1, source_target_pairs={{0,32},{32,0},{64,96},{96,64},{128,160},{160,128},{192,224},{224,1... | collective-permute-start | bytes 884744 | tf_op jit(solution)/shard_map/ppermute | solution.py:429
  96.4 9.2 %collective-permute-start.15 = (bf16[8,768,128]{2,1,0:T(8,128)(2,1)}, bf16[8,768,128]{2,1,0:T(8,128)(2,1)S(1)}, u32[]{:S(2)}, u32[]{:S(2)}) collective-permute-start(bf16[8,768,128]{2,1,0:T(8,128)(2,1)} %get-tuple-element.51), channel_id=1, source_target_pairs={{0,32},{32,0},{64,96},{96,64},{128,160},{160,128},{192,224},{224,1... | collective-permute-start | bytes 4718600 | tf_op jit(solution)/shard_map/ppermute | solution.py:429
  106.9 49.8 %all-to-all-start.1 = ((bf16[32,8,3200]{2,1,0:T(8,128)(2,1)}), bf16[32,8,3200]{2,1,0:T(8,128)(2,1)S(1)}, u32[]{:S(2)}, u32[]{:S(2)}) async-start(bf16[32,8,3200]{2,1,0:T(8,128)(2,1)} %bitcast.17), calls=%async_computation.1 | async-start | bytes 3276800 | tf_op jit(solution)/shard_map/all_to_all | solution.py:409
  112.6 23.1 %collective-permute-start.16 = (bf16[768,128]{1,0:T(8,128)(2,1)}, bf16[768,128]{1,0:T(8,128)(2,1)S(1)}, u32[]{:S(2)}, u32[]{:S(2)}) collective-permute-start(bf16[768,128]{1,0:T(8,128)(2,1)} %get-tuple-element.65), channel_id=1, source_target_pairs={{0,256},{32,288},{64,320},{96,352},{128,384},{160,416},{192,448},{... | collective-permute-start | bytes 589832 | tf_op jit(solution)/shard_map/ppermute | solution.py:426
  120.0 22.8 %collective-permute-start.17 = (bf16[768,128]{1,0:T(8,128)(2,1)}, bf16[768,128]{1,0:T(8,128)(2,1)S(1)}, u32[]{:S(2)}, u32[]{:S(2)}) collective-permute-start(bf16[768,128]{1,0:T(8,128)(2,1)} %get-tuple-element.66), channel_id=1, source_target_pairs={{0,192},{32,224},{64,256},{96,288},{128,320},{160,352},{192,384},{... | collective-permute-start | bytes 589832 | tf_op jit(solution)/shard_map/ppermute | solution.py:426
  122.6 22.2 %collective-permute-start.18 = (bf16[768,128]{1,0:T(8,128)(2,1)S(1)}, bf16[768,128]{1,0:T(8,128)(2,1)S(1)}, u32[]{:S(2)}, u32[]{:S(2)}) collective-permute-start(bf16[768,128]{1,0:T(8,128)(2,1)S(1)} %copy-done.22), channel_id=1, source_target_pairs={{0,320},{32,352},{64,384},{96,416},{128,448},{160,480},{192,0},{22... | collective-permute-start | bytes 589832 | tf_op jit(solution)/shard_map/ppermute | solution.py:426
  128.3 19.3 %collective-permute-start.19 = (bf16[768,128]{1,0:T(8,128)(2,1)S(1)}, bf16[768,128]{1,0:T(8,128)(2,1)S(1)}, u32[]{:S(2)}, u32[]{:S(2)}) collective-permute-start(bf16[768,128]{1,0:T(8,128)(2,1)S(1)} %copy-done.21), channel_id=1, source_target_pairs={{0,128},{32,160},{64,192},{96,224},{128,256},{160,288},{192,320},{... | collective-permute-start | bytes 589832 | tf_op jit(solution)/shard_map/ppermute | solution.py:426
  130.9 20.6 %collective-permute-start.20 = (bf16[768,128]{1,0:T(8,128)(2,1)S(1)}, bf16[768,128]{1,0:T(8,128)(2,1)S(1)}, u32[]{:S(2)}, u32[]{:S(2)}) collective-permute-start(bf16[768,128]{1,0:T(8,128)(2,1)S(1)} %copy-done.20), channel_id=1, source_target_pairs={{0,384},{32,416},{64,448},{96,480},{128,0},{160,32},{192,64},{224,... | collective-permute-start | bytes 589832 | tf_op jit(solution)/shard_map/ppermute | solution.py:426
  135.7 18.9 %collective-permute-start.21 = (bf16[768,128]{1,0:T(8,128)(2,1)S(1)}, bf16[768,128]{1,0:T(8,128)(2,1)S(1)}, u32[]{:S(2)}, u32[]{:S(2)}) collective-permute-start(bf16[768,128]{1,0:T(8,128)(2,1)S(1)} %copy-done.19), channel_id=1, source_target_pairs={{0,64},{32,96},{64,128},{96,160},{128,192},{160,224},{192,256},{22... | collective-permute-start | bytes 589832 | tf_op jit(solution)/shard_map/ppermute | solution.py:426
  142.8 13.0 %collective-permute-start.22 = (bf16[768,128]{1,0:T(8,128)(2,1)S(1)}, bf16[768,128]{1,0:T(8,128)(2,1)S(1)}, u32[]{:S(2)}, u32[]{:S(2)}) collective-permute-start(bf16[768,128]{1,0:T(8,128)(2,1)S(1)} %copy-done.18), channel_id=1, source_target_pairs={{0,448},{32,480},{64,0},{96,32},{128,64},{160,96},{192,128},{224,1... | collective-permute-start | bytes 589832 | tf_op jit(solution)/shard_map/ppermute | solution.py:426
  (24 other events, 497.8 us)

commit v3 on v2

--- a/solution.py
+++ b/solution.py
@@ -508,14 +508,6 @@
     back = exchange(returned)
     far_first = sorted(range(1, ny), key=lambda d: -min(d, ny - d))
     terms = [sums[0]] + [along_y(sums[d], d) for d in far_first]
-    gate_grad, up_grad = call(
-        finish_weights_kernel,
-        (sds((width // dp, hidden), f32),) * 2,
-        [vmem] * (1 + ny),
-        (vmem, vmem),
-        (width * hidden * 2, 4 * width * hidden),
-        name="finish_weights",
-    )(decay, *terms)
     token_grad, prob_grad = call(
         finish_tokens_kernel,
         (sds((count, width), bf16), sds((2, count), bf16)),
@@ -525,6 +517,15 @@
         name="finish_tokens",
         mib=16,
     )(targets, place_left, place_right, back)
+    decay, prob_grad = lax.optimization_barrier((decay, prob_grad))
+    gate_grad, up_grad = call(
+        finish_weights_kernel,
+        (sds((width // dp, hidden), f32),) * 2,
+        [vmem] * (1 + ny),
+        (vmem, vmem),
+        (width * hidden * 2, 4 * width * hidden),
+        name="finish_weights",
+    )(decay, *terms)
     return token_grad, prob_grad.T, gate_grad[None], up_grad[None]
 
 

time: 159 us -> 159 us (level)
  waiting for transfers between devices: 35.6 us -> 33.4 us
    ppermute x14, waiting for transfers between devices: 24.6 us -> 17.4 us  [along_y(): return lax.ppermute(x, 'dp', moves)]
    all_to_all x2, waiting for transfers between devices: 9.28 us -> 14.3 us  [exchange(): lax.all_to_all(blocks, 'expert', split_axis=0, concat_axis=0, tiled=True)]
  transfers between devices with their start and end apart: 25 -> 25, of which waited for: 11 -> 10; matrix products, arithmetic and copies ran while one was open for 0% -> 0% of each run, Pallas kernels for 8% -> 8%
where the time goes in v3:
time: 159 us; the launch traced here: 158 us
  starting transfers between devices  95.5 us (60%)
  waiting for transfers between devices  33.4 us (21%)
  Pallas kernels  26 us (16%)
  local copies, waits for them, and re-layouts  1.59 us (1%)
    ppermute x14, starting transfers between devices, along_y(): return lax.ppermute(x, 'dp', moves)  49.8 us
    ppermute x9, starting transfers between devices, across(): return lax.ppermute(x, 'dp', [(i, i ^ 1) for i in range(dp)])  26.4 us
    pallas_call x8, Pallas kernels, run(): return kernel_call(*pinned)  26 us
    all_to_all x2, starting transfers between devices, exchange(): lax.all_to_all(blocks, 'expert', split_axis=0, concat_axis=0, tiled=True)  19.4 us
    ppermute x14, waiting for transfers between devices, along_y(): return lax.ppermute(x, 'dp', moves)  17.4 us
    all_to_all x2, waiting for transfers between devices, exchange(): lax.all_to_all(blocks, 'expert', split_axis=0, concat_axis=0, tiled=True)  14.3 us
  transfers between devices with their start and end apart: 25, of which 10 were waited for; matrix products, arithmetic and copies ran while one was open for 0% of the time, Pallas kernels for 8%

profile of v3, /device:TPU:1, one launch (start us, length us, event | category | flops | bytes accessed | tf_op | source)
XLA Modules:
  0.0 157.6 jit_solution(11054481698938864014)
XLA Ops:
  0.6 3.3 %place.1 = (bf16[256,6144]{1,0:T(8,128)(2,1)}, f32[8,128]{1,0:T(8,128)}) custom-call(s32[2,128]{1,0:T(2,128)} %bitcast.26, bf16[2,128]{1,0:T(2,128)(2,1)} %bitcast.27, bf16[128,2048]{1,0:T(8,128)(2,1)} %tokens_hbm.1, bf16[128,2048]{1,0:T(8,128)(2,1)} %grads_hbm.1), custom_call_target="tpu_custom_call" | custom-call | flops 671088640 | bytes 5242880 | tf_op jit(solution)/shard_map/place/pallas_call | solution.py:45
  4.0 13.7 %all-to-all-start = ((bf16[32,8,6144]{2,1,0:T(8,128)(2,1)}), bf16[32,8,6144]{2,1,0:T(8,128)(2,1)S(1)}, u32[]{:S(2)}, u32[]{:S(2)}) async-start(bf16[32,8,6144]{2,1,0:T(8,128)(2,1)} %bitcast.17), calls=%async_computation | async-start | bytes 6291456 | tf_op jit(solution)/shard_map/all_to_all | solution.py:409
  17.7 3.0 %mask.1 = (bf16[128,1152]{1,0:T(8,128)(2,1)}, f32[128,768]{1,0:T(8,128)}) custom-call(bf16[128,384]{1,0:T(8,128)(2,1)} %bitcast.18, bf16[128,384]{1,0:T(8,128)(2,1)} %bitcast.19, bf16[384,128]{1,0:T(8,128)(2,1)} %bitcast.20, s32[32,384]{1,0:T(8,128)} %bitcast.21, s32[32,384]{1,0:T(8,128)} %bitcast.22, s32[96,128]{1,0:T(8,128)} %bitcast.23), custom_call_target="tpu_custom_call" | custom-call | flops 78643200 | bytes 294912 | tf_op jit(solution)/shard_map/mask/pallas_call | solution.py:45
  20.7 3.2 %collective-permute-start = (bf16[128,1152]{1,0:T(8,128)(2,1)}, bf16[128,1152]{1,0:T(8,128)(2,1)S(1)}, u32[]{:S(2)}, u32[]{:S(2)}) collective-permute-start(bf16[128,1152]{1,0:T(8,128)(2,1)} %get-tuple-element.42.refs_0_), channel_id=1, source_target_pairs={{0,64},{32,96},{64,128},{96,160},{128,192},{160,224},{192,256},{22... | collective-permute-start | bytes 884744 | tf_op jit(solution)/shard_map/ppermute | solution.py:426
  23.9 3.8 %collective-permute-start.4 = (bf16[128,1152]{1,0:T(8,128)(2,1)}, bf16[128,1152]{1,0:T(8,128)(2,1)S(1)}, u32[]{:S(2)}, u32[]{:S(2)}) collective-permute-start(bf16[128,1152]{1,0:T(8,128)(2,1)} %get-tuple-element.42.refs_0_), channel_id=1, source_target_pairs={{0,448},{32,480},{64,0},{96,32},{128,64},{160,96},{192,128},{224,1... | collective-permute-start | bytes 884744 | tf_op jit(solution)/shard_map/ppermute | solution.py:426
  27.7 4.7 %collective-permute-done.refs_1_ = bf16[128,1152]{1,0:T(8,128)(2,1)S(1)} collective-permute-done((bf16[128,1152]{1,0:T(8,128)(2,1)}, bf16[128,1152]{1,0:T(8,128)(2,1)S(1)}, u32[]{:S(2)}, u32[]{:S(2)}) %collective-permute-start) | collective-permute-done | bytes 294944 | tf_op jit(solution)/shard_map/ppermute | solution.py:426
  34.3 4.6 %collective-permute-start.5 = (bf16[128,1152]{1,0:T(8,128)(2,1)S(1)}, bf16[128,1152]{1,0:T(8,128)(2,1)S(1)}, u32[]{:S(2)}, u32[]{:S(2)}) collective-permute-start(bf16[128,1152]{1,0:T(8,128)(2,1)S(1)} %collective-permute-done.4.refs_5_), channel_id=1, source_target_pairs={{0,448},{32,480},{64,0},{96,32},{128,64},{160,96},{192,128},{224,1... | collective-permute-start | bytes 884744 | tf_op jit(solution)/shard_map/ppermute | solution.py:426
  38.9 3.5 %collective-permute-done.1.refs_2_ = bf16[128,1152]{1,0:T(8,128)(2,1)S(1)} collective-permute-done((bf16[128,1152]{1,0:T(8,128)(2,1)S(1)}, bf16[128,1152]{1,0:T(8,128)(2,1)S(1)}, u32[]{:S(2)}, u32[]{:S(2)}) %collective-permute-start.1) | collective-permute-done | bytes 294944 | tf_op jit(solution)/shard_map/ppermute | solution.py:426
  44.3 4.4 %collective-permute-start.7 = (bf16[128,1152]{1,0:T(8,128)(2,1)}, bf16[128,1152]{1,0:T(8,128)(2,1)S(1)}, u32[]{:S(2)}, u32[]{:S(2)}) collective-permute-start(bf16[128,1152]{1,0:T(8,128)(2,1)} %get-tuple-element.42.refs_0_), channel_id=1, source_target_pairs={{0,32},{32,0},{64,96},{96,64},{128,160},{160,128},{192,224},{224,1... | collective-permute-start | bytes 884744 | tf_op jit(solution)/shard_map/ppermute | solution.py:429
  53.1 4.9 %collective-permute-start.6 = (bf16[128,1152]{1,0:T(8,128)(2,1)S(1)}, bf16[128,1152]{1,0:T(8,128)(2,1)S(1)}, u32[]{:S(2)}, u32[]{:S(2)}) collective-permute-start(bf16[128,1152]{1,0:T(8,128)(2,1)S(1)} %collective-permute-done.5.refs_6_), channel_id=1, source_target_pairs={{0,448},{32,480},{64,0},{96,32},{128,64},{160,96},{192,128},{224,1... | collective-permute-start | bytes 884744 | tf_op jit(solution)/shard_map/ppermute | solution.py:426
  69.4 3.0 %collective-permute-start.11 = (bf16[128,1152]{1,0:T(8,128)(2,1)S(1)}, bf16[128,1152]{1,0:T(8,128)(2,1)S(1)}, u32[]{:S(2)}, u32[]{:S(2)}) collective-permute-start(bf16[128,1152]{1,0:T(8,128)(2,1)S(1)} %collective-permute-done.3.refs_4_), channel_id=1, source_target_pairs={{0,32},{32,0},{64,96},{96,64},{128,160},{160,128},{192,224},{224,1... | collective-permute-start | bytes 884744 | tf_op jit(solution)/shard_map/ppermute | solution.py:429
  74.3 5.6 %assemble.1 = (bf16[2048,768]{1,0:T(8,128)(2,1)}, bf16[2048,384]{1,0:T(8,128)(2,1)}, bf16[768,2048]{1,0:T(8,128)(2,1)}, bf16[128,512]{1,0:T(8,128)(2,1)S(1)}, bf16[128,512]{1,0:T(8,128)(2,1)S(1)}) custom-call(f32[8,128]{1,0:T(8,128)S(1)} %copy-done.4, bf16[128,1152]{1,0:T(8,128)(2,1)} %get-tuple-element.42.refs_0_, bf16[128,1152]{1,0:T(8,128)(2,1)} %copy-done.5, ...), custom_call_target="tpu_custom_call" | custom-call | flops 327680 | bytes 4718592 | tf_op jit(solution)/shard_map/assemble/pallas_call | solution.py:45
  79.9 9.3 %all-to-all-done = bf16[32,8,6144]{2,1,0:T(8,128)(2,1)S(1)} async-done(((bf16[32,8,6144]{2,1,0:T(8,128)(2,1)}), bf16[32,8,6144]{2,1,0:T(8,128)(2,1)S(1)}, u32[]{:S(2)}, u32[]{:S(2)}) %all-to-all-start) | async-done | bytes 3145760 | tf_op jit(solution)/shard_map/all_to_all | solution.py:409
  89.2 7.1 %delta.1 = (bf16[384,768]{1,0:T(8,128)(2,1)S(1)}, bf16[384,128]{1,0:T(8,128)(2,1)S(1)}, bf16[768,2048]{1,0:T(8,128)(2,1)S(1)}, bf16[8,768,128]{2,1,0:T(8,128)(2,1)S(1)}, bf16[8,768,128]{2,1,0:T(8,128)(2,1)}) custom-call(bf16[256,6144]{1,0:T(8,128)(2,1)S(1)} %bitcast.16, bf16[2048,768]{1,0:T(8,128)(2,1)} %get-tuple-element.46.weight_hbm, ...), custom_call_target="tpu_custom_call" | custom-call | flops 3019898880 | bytes 6291456 | tf_op jit(solution)/shard_map/delta/pallas_call | solution.py:45
  96.3 6.0 %collective-permute-start.15 = (bf16[8,768,128]{2,1,0:T(8,128)(2,1)}, bf16[8,768,128]{2,1,0:T(8,128)(2,1)S(1)}, u32[]{:S(2)}, u32[]{:S(2)}) collective-permute-start(bf16[8,768,128]{2,1,0:T(8,128)(2,1)} %get-tuple-element.53), channel_id=1, source_target_pairs={{0,32},{32,0},{64,96},{96,64},{128,160},{160,128},{192,224},{224,1... | collective-permute-start | bytes 4718600 | tf_op jit(solution)/shard_map/ppermute | solution.py:429
  102.3 2.6 %slot_grad.1 = bf16[256,3200]{1,0:T(8,128)(2,1)} custom-call(bf16[384,768]{1,0:T(8,128)(2,1)S(1)} %get-tuple-element.49.delta_ref, bf16[384,128]{1,0:T(8,128)(2,1)S(1)} %get-tuple-element.50.prob_ref, bf16[768,2048]{1,0:T(8,128)(2,1)S(1)} %get-tuple-element.51.turned_ref), custom_call_target="tpu_custom_call" | custom-call | flops 1207959552 | bytes 6291456 | tf_op jit(solution)/shard_map/slot_grad/pallas_call | solution.py:45
  106.8 5.6 %all-to-all-start.1 = ((bf16[32,8,3200]{2,1,0:T(8,128)(2,1)}), bf16[32,8,3200]{2,1,0:T(8,128)(2,1)S(1)}, u32[]{:S(2)}, u32[]{:S(2)}) async-start(bf16[32,8,3200]{2,1,0:T(8,128)(2,1)} %bitcast.10), calls=%async_computation.1 | async-start | bytes 3276800 | tf_op jit(solution)/shard_map/all_to_all | solution.py:409
  112.5 7.5 %collective-permute-start.16 = (bf16[768,128]{1,0:T(8,128)(2,1)S(1)}, bf16[768,128]{1,0:T(8,128)(2,1)S(1)}, u32[]{:S(2)}, u32[]{:S(2)}) collective-permute-start(bf16[768,128]{1,0:T(8,128)(2,1)S(1)} %copy-done.20), channel_id=1, source_target_pairs={{0,256},{32,288},{64,320},{96,352},{128,384},{160,416},{192,448},{... | collective-permute-start | bytes 589832 | tf_op jit(solution)/shard_map/ppermute | solution.py:426
  120.0 2.6 %collective-permute-start.17 = (bf16[768,128]{1,0:T(8,128)(2,1)}, bf16[768,128]{1,0:T(8,128)(2,1)S(1)}, u32[]{:S(2)}, u32[]{:S(2)}) collective-permute-start(bf16[768,128]{1,0:T(8,128)(2,1)} %get-tuple-element.70), channel_id=1, source_target_pairs={{0,192},{32,224},{64,256},{96,288},{128,320},{160,352},{192,384},{... | collective-permute-start | bytes 589832 | tf_op jit(solution)/shard_map/ppermute | solution.py:426
  122.6 5.7 %collective-permute-start.18 = (bf16[768,128]{1,0:T(8,128)(2,1)}, bf16[768,128]{1,0:T(8,128)(2,1)S(1)}, u32[]{:S(2)}, u32[]{:S(2)}) collective-permute-start(bf16[768,128]{1,0:T(8,128)(2,1)} %get-tuple-element.71), channel_id=1, source_target_pairs={{0,320},{32,352},{64,384},{96,416},{128,448},{160,480},{192,0},{22... | collective-permute-start | bytes 589832 | tf_op jit(solution)/shard_map/ppermute | solution.py:426
  128.3 2.6 %collective-permute-start.19 = (bf16[768,128]{1,0:T(8,128)(2,1)}, bf16[768,128]{1,0:T(8,128)(2,1)S(1)}, u32[]{:S(2)}, u32[]{:S(2)}) collective-permute-start(bf16[768,128]{1,0:T(8,128)(2,1)} %get-tuple-element.72), channel_id=1, source_target_pairs={{0,128},{32,160},{64,192},{96,224},{128,256},{160,288},{192,320},{... | collective-permute-start | bytes 589832 | tf_op jit(solution)/shard_map/ppermute | solution.py:426
  130.9 4.8 %collective-permute-start.20 = (bf16[768,128]{1,0:T(8,128)(2,1)}, bf16[768,128]{1,0:T(8,128)(2,1)S(1)}, u32[]{:S(2)}, u32[]{:S(2)}) collective-permute-start(bf16[768,128]{1,0:T(8,128)(2,1)} %get-tuple-element.73), channel_id=1, source_target_pairs={{0,384},{32,416},{64,448},{96,480},{128,0},{160,32},{192,64},{224,... | collective-permute-start | bytes 589832 | tf_op jit(solution)/shard_map/ppermute | solution.py:426
  138.2 5.1 %collective-permute-done.17.refs_2_ = bf16[768,128]{1,0:T(8,128)(2,1)S(1)} collective-permute-done((bf16[768,128]{1,0:T(8,128)(2,1)}, bf16[768,128]{1,0:T(8,128)(2,1)S(1)}, u32[]{:S(2)}, u32[]{:S(2)}) %collective-permute-start.17) | collective-permute-done | bytes 196640 | tf_op jit(solution)/shard_map/ppermute | solution.py:426
  145.3 5.0 %all-to-all-done.1 = bf16[32,8,3200]{2,1,0:T(8,128)(2,1)S(1)} async-done(((bf16[32,8,3200]{2,1,0:T(8,128)(2,1)}), bf16[32,8,3200]{2,1,0:T(8,128)(2,1)S(1)}, u32[]{:S(2)}, u32[]{:S(2)}) %all-to-all-start.1) | async-done | bytes 1638432 | tf_op jit(solution)/shard_map/all_to_all | solution.py:409
  (76 shorter events, 34.8 us)
Async XLA Ops:
  4.0 85.2 %all-to-all-start = ((bf16[32,8,6144]{2,1,0:T(8,128)(2,1)}), bf16[32,8,6144]{2,1,0:T(8,128)(2,1)S(1)}, u32[]{:S(2)}, u32[]{:S(2)}) async-start(bf16[32,8,6144]{2,1,0:T(8,128)(2,1)} %bitcast.17), calls=%async_computation | async-start | bytes 6291456 | tf_op jit(solution)/shard_map/all_to_all | solution.py:409
  20.7 11.7 %collective-permute-start = (bf16[128,1152]{1,0:T(8,128)(2,1)}, bf16[128,1152]{1,0:T(8,128)(2,1)S(1)}, u32[]{:S(2)}, u32[]{:S(2)}) collective-permute-start(bf16[128,1152]{1,0:T(8,128)(2,1)} %get-tuple-element.42.refs_0_), channel_id=1, source_target_pairs={{0,64},{32,96},{64,128},{96,160},{128,192},{160,224},{192,256},{22... | collective-permute-start | bytes 884744 | tf_op jit(solution)/shard_map/ppermute | solution.py:426
  23.9 10.4 %collective-permute-start.4 = (bf16[128,1152]{1,0:T(8,128)(2,1)}, bf16[128,1152]{1,0:T(8,128)(2,1)S(1)}, u32[]{:S(2)}, u32[]{:S(2)}) collective-permute-start(bf16[128,1152]{1,0:T(8,128)(2,1)} %get-tuple-element.42.refs_0_), channel_id=1, source_target_pairs={{0,448},{32,480},{64,0},{96,32},{128,64},{160,96},{192,128},{224,1... | collective-permute-start | bytes 884744 | tf_op jit(solution)/shard_map/ppermute | solution.py:426
  32.4 10.0 %collective-permute-start.1 = (bf16[128,1152]{1,0:T(8,128)(2,1)S(1)}, bf16[128,1152]{1,0:T(8,128)(2,1)S(1)}, u32[]{:S(2)}, u32[]{:S(2)}) collective-permute-start(bf16[128,1152]{1,0:T(8,128)(2,1)S(1)} %collective-permute-done.refs_1_), channel_id=1, source_target_pairs={{0,64},{32,96},{64,128},{96,160},{128,192},{160,224},{192,256},{22... | collective-permute-start | bytes 884744 | tf_op jit(solution)/shard_map/ppermute | solution.py:426
  34.3 18.8 %collective-permute-start.5 = (bf16[128,1152]{1,0:T(8,128)(2,1)S(1)}, bf16[128,1152]{1,0:T(8,128)(2,1)S(1)}, u32[]{:S(2)}, u32[]{:S(2)}) collective-permute-start(bf16[128,1152]{1,0:T(8,128)(2,1)S(1)} %collective-permute-done.4.refs_5_), channel_id=1, source_target_pairs={{0,448},{32,480},{64,0},{96,32},{128,64},{160,96},{192,128},{224,1... | collective-permute-start | bytes 884744 | tf_op jit(solution)/shard_map/ppermute | solution.py:426
  42.4 15.5 %collective-permute-start.2 = (bf16[128,1152]{1,0:T(8,128)(2,1)S(1)}, bf16[128,1152]{1,0:T(8,128)(2,1)S(1)}, u32[]{:S(2)}, u32[]{:S(2)}) collective-permute-start(bf16[128,1152]{1,0:T(8,128)(2,1)S(1)} %collective-permute-done.1.refs_2_), channel_id=1, source_target_pairs={{0,64},{32,96},{64,128},{96,160},{128,192},{160,224},{192,256},{22... | collective-permute-start | bytes 884744 | tf_op jit(solution)/shard_map/ppermute | solution.py:426
  44.3 15.6 %collective-permute-start.7 = (bf16[128,1152]{1,0:T(8,128)(2,1)}, bf16[128,1152]{1,0:T(8,128)(2,1)S(1)}, u32[]{:S(2)}, u32[]{:S(2)}) collective-permute-start(bf16[128,1152]{1,0:T(8,128)(2,1)} %get-tuple-element.42.refs_0_), channel_id=1, source_target_pairs={{0,32},{32,0},{64,96},{96,64},{128,160},{160,128},{192,224},{224,1... | collective-permute-start | bytes 884744 | tf_op jit(solution)/shard_map/ppermute | solution.py:429
  48.7 13.4 %collective-permute-start.12 = (bf16[128,1152]{1,0:T(8,128)(2,1)S(1)}, bf16[128,1152]{1,0:T(8,128)(2,1)S(1)}, u32[]{:S(2)}, u32[]{:S(2)}) collective-permute-start(bf16[128,1152]{1,0:T(8,128)(2,1)S(1)} %collective-permute-done.4.refs_5_), channel_id=1, source_target_pairs={{0,32},{32,0},{64,96},{96,64},{128,160},{160,128},{192,224},{224,1... | collective-permute-start | bytes 884744 | tf_op jit(solution)/shard_map/ppermute | solution.py:429
  50.6 13.6 %collective-permute-start.8 = (bf16[128,1152]{1,0:T(8,128)(2,1)S(1)}, bf16[128,1152]{1,0:T(8,128)(2,1)S(1)}, u32[]{:S(2)}, u32[]{:S(2)}) collective-permute-start(bf16[128,1152]{1,0:T(8,128)(2,1)S(1)} %collective-permute-done.refs_1_), channel_id=1, source_target_pairs={{0,32},{32,0},{64,96},{96,64},{128,160},{160,128},{192,224},{224,1... | collective-permute-start | bytes 884744 | tf_op jit(solution)/shard_map/ppermute | solution.py:429
  53.1 13.4 %collective-permute-start.6 = (bf16[128,1152]{1,0:T(8,128)(2,1)S(1)}, bf16[128,1152]{1,0:T(8,128)(2,1)S(1)}, u32[]{:S(2)}, u32[]{:S(2)}) collective-permute-start(bf16[128,1152]{1,0:T(8,128)(2,1)S(1)} %collective-permute-done.5.refs_6_), channel_id=1, source_target_pairs={{0,448},{32,480},{64,0},{96,32},{128,64},{160,96},{192,128},{224,1... | collective-permute-start | bytes 884744 | tf_op jit(solution)/shard_map/ppermute | solution.py:426
  58.0 11.4 %collective-permute-start.3 = (bf16[128,1152]{1,0:T(8,128)(2,1)S(1)}, bf16[128,1152]{1,0:T(8,128)(2,1)S(1)}, u32[]{:S(2)}, u32[]{:S(2)}) collective-permute-start(bf16[128,1152]{1,0:T(8,128)(2,1)S(1)} %collective-permute-done.2.refs_3_), channel_id=1, source_target_pairs={{0,64},{32,96},{64,128},{96,160},{128,192},{160,224},{192,256},{22... | collective-permute-start | bytes 884744 | tf_op jit(solution)/shard_map/ppermute | solution.py:426
  59.9 12.5 %collective-permute-start.13 = (bf16[128,1152]{1,0:T(8,128)(2,1)S(1)}, bf16[128,1152]{1,0:T(8,128)(2,1)S(1)}, u32[]{:S(2)}, u32[]{:S(2)}) collective-permute-start(bf16[128,1152]{1,0:T(8,128)(2,1)S(1)} %collective-permute-done.5.refs_6_), channel_id=1, source_target_pairs={{0,32},{32,0},{64,96},{96,64},{128,160},{160,128},{192,224},{224,1... | collective-permute-start | bytes 884744 | tf_op jit(solution)/shard_map/ppermute | solution.py:429
  62.1 10.3 %collective-permute-start.9 = (bf16[128,1152]{1,0:T(8,128)(2,1)S(1)}, bf16[128,1152]{1,0:T(8,128)(2,1)S(1)}, u32[]{:S(2)}, u32[]{:S(2)}) collective-permute-start(bf16[128,1152]{1,0:T(8,128)(2,1)S(1)} %collective-permute-done.1.refs_2_), channel_id=1, source_target_pairs={{0,32},{32,0},{64,96},{96,64},{128,160},{160,128},{192,224},{224,1... | collective-permute-start | bytes 884744 | tf_op jit(solution)/shard_map/ppermute | solution.py:429
  64.3 8.2 %collective-permute-start.10 = (bf16[128,1152]{1,0:T(8,128)(2,1)S(1)}, bf16[128,1152]{1,0:T(8,128)(2,1)S(1)}, u32[]{:S(2)}, u32[]{:S(2)}) collective-permute-start(bf16[128,1152]{1,0:T(8,128)(2,1)S(1)} %collective-permute-done.2.refs_3_), channel_id=1, source_target_pairs={{0,32},{32,0},{64,96},{96,64},{128,160},{160,128},{192,224},{224,1... | collective-permute-start | bytes 884744 | tf_op jit(solution)/shard_map/ppermute | solution.py:429
  66.5 5.9 %collective-permute-start.14 = (bf16[128,1152]{1,0:T(8,128)(2,1)S(1)}, bf16[128,1152]{1,0:T(8,128)(2,1)S(1)}, u32[]{:S(2)}, u32[]{:S(2)}) collective-permute-start(bf16[128,1152]{1,0:T(8,128)(2,1)S(1)} %collective-permute-done.6.refs_7_), channel_id=1, source_target_pairs={{0,32},{32,0},{64,96},{96,64},{128,160},{160,128},{192,224},{224,1... | collective-permute-start | bytes 884744 | tf_op jit(solution)/shard_map/ppermute | solution.py:429
  96.3 9.2 %collective-permute-start.15 = (bf16[8,768,128]{2,1,0:T(8,128)(2,1)}, bf16[8,768,128]{2,1,0:T(8,128)(2,1)S(1)}, u32[]{:S(2)}, u32[]{:S(2)}) collective-permute-start(bf16[8,768,128]{2,1,0:T(8,128)(2,1)} %get-tuple-element.53), channel_id=1, source_target_pairs={{0,32},{32,0},{64,96},{96,64},{128,160},{160,128},{192,224},{224,1... | collective-permute-start | bytes 4718600 | tf_op jit(solution)/shard_map/ppermute | solution.py:429
  106.8 43.5 %all-to-all-start.1 = ((bf16[32,8,3200]{2,1,0:T(8,128)(2,1)}), bf16[32,8,3200]{2,1,0:T(8,128)(2,1)S(1)}, u32[]{:S(2)}, u32[]{:S(2)}) async-start(bf16[32,8,3200]{2,1,0:T(8,128)(2,1)} %bitcast.10), calls=%async_computation.1 | async-start | bytes 3276800 | tf_op jit(solution)/shard_map/all_to_all | solution.py:409
  112.5 23.2 %collective-permute-start.16 = (bf16[768,128]{1,0:T(8,128)(2,1)S(1)}, bf16[768,128]{1,0:T(8,128)(2,1)S(1)}, u32[]{:S(2)}, u32[]{:S(2)}) collective-permute-start(bf16[768,128]{1,0:T(8,128)(2,1)S(1)} %copy-done.20), channel_id=1, source_target_pairs={{0,256},{32,288},{64,320},{96,352},{128,384},{160,416},{192,448},{... | collective-permute-start | bytes 589832 | tf_op jit(solution)/shard_map/ppermute | solution.py:426
  120.0 23.4 %collective-permute-start.17 = (bf16[768,128]{1,0:T(8,128)(2,1)}, bf16[768,128]{1,0:T(8,128)(2,1)S(1)}, u32[]{:S(2)}, u32[]{:S(2)}) collective-permute-start(bf16[768,128]{1,0:T(8,128)(2,1)} %get-tuple-element.70), channel_id=1, source_target_pairs={{0,192},{32,224},{64,256},{96,288},{128,320},{160,352},{192,384},{... | collective-permute-start | bytes 589832 | tf_op jit(solution)/shard_map/ppermute | solution.py:426
  122.6 29.9 %collective-permute-start.18 = (bf16[768,128]{1,0:T(8,128)(2,1)}, bf16[768,128]{1,0:T(8,128)(2,1)S(1)}, u32[]{:S(2)}, u32[]{:S(2)}) collective-permute-start(bf16[768,128]{1,0:T(8,128)(2,1)} %get-tuple-element.71), channel_id=1, source_target_pairs={{0,320},{32,352},{64,384},{96,416},{128,448},{160,480},{192,0},{22... | collective-permute-start | bytes 589832 | tf_op jit(solution)/shard_map/ppermute | solution.py:426
  128.3 24.2 %collective-permute-start.19 = (bf16[768,128]{1,0:T(8,128)(2,1)}, bf16[768,128]{1,0:T(8,128)(2,1)S(1)}, u32[]{:S(2)}, u32[]{:S(2)}) collective-permute-start(bf16[768,128]{1,0:T(8,128)(2,1)} %get-tuple-element.72), channel_id=1, source_target_pairs={{0,128},{32,160},{64,192},{96,224},{128,256},{160,288},{192,320},{... | collective-permute-start | bytes 589832 | tf_op jit(solution)/shard_map/ppermute | solution.py:426
  130.9 21.6 %collective-permute-start.20 = (bf16[768,128]{1,0:T(8,128)(2,1)}, bf16[768,128]{1,0:T(8,128)(2,1)S(1)}, u32[]{:S(2)}, u32[]{:S(2)}) collective-permute-start(bf16[768,128]{1,0:T(8,128)(2,1)} %get-tuple-element.73), channel_id=1, source_target_pairs={{0,384},{32,416},{64,448},{96,480},{128,0},{160,32},{192,64},{224,... | collective-permute-start | bytes 589832 | tf_op jit(solution)/shard_map/ppermute | solution.py:426
  135.7 18.4 %collective-permute-start.21 = (bf16[768,128]{1,0:T(8,128)(2,1)}, bf16[768,128]{1,0:T(8,128)(2,1)S(1)}, u32[]{:S(2)}, u32[]{:S(2)}) collective-permute-start(bf16[768,128]{1,0:T(8,128)(2,1)} %get-tuple-element.74), channel_id=1, source_target_pairs={{0,64},{32,96},{64,128},{96,160},{128,192},{160,224},{192,256},{22... | collective-permute-start | bytes 589832 | tf_op jit(solution)/shard_map/ppermute | solution.py:426
  143.4 12.4 %collective-permute-start.22 = (bf16[768,128]{1,0:T(8,128)(2,1)}, bf16[768,128]{1,0:T(8,128)(2,1)}, u32[]{:S(2)}, u32[]{:S(2)}) collective-permute-start(bf16[768,128]{1,0:T(8,128)(2,1)} %get-tuple-element.75), channel_id=1, source_target_pairs={{0,448},{32,480},{64,0},{96,32},{128,64},{160,96},{192,128},{224,1... | collective-permute-start | bytes 589832 | tf_op jit(solution)/shard_map/ppermute | solution.py:426
  (22 other events, 383.6 us)
